TPU v7x, 256 devices: a whole 4x4x8 slice. The times are simulated.
256 devices in a mesh: chan: 64 (over y, z, x_lo), off: 4 (over x_hi, core).
Axes of the slice: x: 4 (x_hi: 2, x_lo: 2; x = x_hi * 2 + x_lo), y: 4, z: 8, core: 2. Of those that a mesh axis runs over, the one named last changes fastest.
Arguments:
- spectra: bfloat16 [16384, 128, 128], P('chan', 'off'), may hold values from -40 to 40
- pair_bins: int32 [64, 3, 256, 256], P('chan'), may hold values from 0 to 255, as said below
Outputs:
- stacked: float32 [256, 128], P(('chan', 'off'))
Inputs may be any that keep to these rules, and one draw needn't show every extreme that they name: `pair_bins`: labels follow the fiber's geometry: a label is d * 4 + g, where d is a class of the distance along the fiber between the two channels and g the segment of the fiber that holds the second channel.
All inputs are finite; a program needn't handle non-finite values.
Results may differ from a plain program's by a relative error of at most 0.0003.
Values may be sent and summed in bfloat16 or wider, within the bound.
A program may use at most 128 MiB of HBM per device.

v0:
```python
import math

import jax
import jax.numpy as jnp
from jax import lax
from jax.sharding import PartitionSpec as P

BINS_DEV = 1


def from_behind(value, axis, steps):
    count = lax.axis_size(axis)
    pairs = [(source, (source + steps) % count) for source in range(count)]
    return lax.ppermute(value, axis, pairs)


def whiten(spectra):
    values = spectra.astype(jnp.float32)
    meansq = jnp.mean(values * values, axis=-1, keepdims=True)
    return (values * lax.rsqrt(meansq + 1e-05)).astype(jnp.bfloat16)


def lag_table(freqs, nfreq, lags):
    shifts = jnp.arange(lags, dtype=jnp.int32) - lags // 2
    phase = jnp.mod(freqs[:, None] * shifts[None, :], 2 * nfreq)
    theta = math.pi * phase.astype(jnp.float32) / nfreq
    return jnp.concatenate([jnp.cos(theta), -jnp.sin(theta)], axis=0)


def cross_pairs(own, other):
    half = own.shape[-1] // 2
    rotated = jnp.concatenate([own[..., half:], -own[..., :half]], axis=-1)
    both = jnp.stack([own, rotated], axis=0)
    cross = jnp.einsum("rifs,jfs->rfij", both, other, preferred_element_type=jnp.float32)
    cross = (cross * (1.0 / half)).astype(jnp.bfloat16)
    return cross.reshape(2 * own.shape[1], own.shape[0], other.shape[0])


def stack_pairs(cross, labels, binned, counts):
    chans = cross.shape[1]
    nbins = binned.shape[1]
    rows = math.gcd(chans, max(1, 2048 // chans))
    bin_ids = jnp.arange(nbins, dtype=jnp.int32)

    def add_block(block_index, carry):
        totals, tallies = carry
        piece = lax.dynamic_slice_in_dim(cross, block_index * rows, rows, 1).reshape(
            cross.shape[0], rows * chans
        )
        marks = lax.dynamic_slice_in_dim(labels, block_index * rows, rows, 0).reshape(rows * chans)
        onehot = marks[:, None] == bin_ids[None, :]
        totals = totals + jnp.dot(
            piece, onehot.astype(jnp.bfloat16), preferred_element_type=jnp.float32
        )
        tallies = tallies + jnp.sum(onehot.astype(jnp.float32), axis=0)
        return (totals, tallies)

    return lax.fori_loop(0, chans // rows, add_block, (binned, counts))


def on_device(spectra, pair_bins):
    span = pair_bins.shape[1] - 1
    freq_local = spectra.shape[1]
    nfreq = freq_local * lax.axis_size("off")
    nbins = BINS_DEV * lax.axis_size("chan") * lax.axis_size("off")
    white = whiten(spectra)
    labels = pair_bins[0]
    binned = jnp.zeros((2 * freq_local, nbins), jnp.float32)
    counts = jnp.zeros((nbins,), jnp.float32)
    for step in range(span + 1):
        partner = white if step == 0 else from_behind(white, "chan", -step)
        cross = cross_pairs(white, partner)
        binned, counts = stack_pairs(cross, labels[step], binned, counts)
    freqs = lax.axis_index("off") * freq_local + jnp.arange(freq_local, dtype=jnp.int32)
    table = lag_table(freqs, nfreq, nfreq)
    contract = (((0,), (0,)), ((), ()))
    partial_traces = lax.dot_general(
        binned, table, contract, precision=lax.Precision.HIGHEST, preferred_element_type=jnp.float32
    )
    traces = lax.psum_scatter(partial_traces, ("chan", "off"), scatter_dimension=0, tiled=True)
    all_counts = lax.psum(counts, "chan")
    start = (lax.axis_index("chan") * lax.axis_size("off") + lax.axis_index("off")) * BINS_DEV
    owned = lax.dynamic_slice_in_dim(all_counts, start, BINS_DEV, 0)
    return traces / jnp.sqrt(jnp.maximum(owned, 1.0))[:, None]


def solution(mesh):
    in_specs = (P("chan", "off", None), P("chan", None, None, None))
    out_specs = P(("chan", "off"), None)
    return jax.shard_map(
        on_device, mesh=mesh, in_specs=in_specs, out_specs=out_specs, check_vma=False
    )
```

profile of v0, /device:TPU:1, one launch (start us, length us, event | category | flops | bytes accessed | tf_op | source)
XLA Modules:
  0.0 554.2 jit_solution(3182692586201974835)
XLA Ops:
  6.5 3.1 fusion.24
  9.7 3.5 fusion.25
  13.1 9.8 %collective-permute-start = (bf16[256,32,128]{2,0,1:T(8,128)(2,1)}, bf16[256,32,128]{2,0,1:T(8,128)(2,1)}, u32[]{:S(2)}, u32[]{:S(2)}) collective-permute-start(bf16[256,32,128]{2,0,1:T(8,128)(2,1)} %fusion.25), channel_id=1, source_target_pairs={{0,252},{4,0},{8,4},{12,8},{16,12},{20,16},{24,20},{28,24},{32,28}... | collective-permute-start | bytes 6291464 | tf_op jit(solution)/shard_map/ppermute | solution.py:14
  23.6 4.9 fusion.41
  28.6 2.5 fusion.46
  31.1 3.4 maximum_bitcast_fusion
  34.5 1.3 copy-done
  35.8 6.2 %fusion.21 = bf16[2,32,256,256]{2,3,0,1:T(8,128)(2,1)} fusion(bf16[256,32,128]{2,0,1:T(8,128)(2,1)} %fusion.25, bf16[1,256,32,128]{3,1,0,2:T(8,128)(2,1)S(1)} %maximum_bitcast_fusion, bf16[1,256,32,128]{3,1,0,2:T(8,128)(2,1)S(1)} %fusion.46), kind=kOutput, calls=%fused_computation.31 | convolution fusion | flops 1090519040 | bytes 14680064 | tf_op jit(solution)/shard_map/rifs,jfs->rfij/dot_general | solution.py:34
  42.0 12.0 %copy.17 = bf16[2,32,256,256]{3,2,1,0:T(8,128)(2,1)} copy(bf16[2,32,256,256]{2,3,0,1:T(8,128)(2,1)} %fusion.21) | data formatting | bytes 16777216 | tf_op jit(solution)/shard_map/convert_element_type | solution.py:35
  54.7 86.3 %while.50 = (s32[]{:T(128)}, f32[64,256]{1,0:T(8,128)S(1)}, f32[256]{0:T(256)S(1)}, bf16[64,256,256]{2,1,0:T(8,128)(2,1)}, s32[256,256]{1,0:T(8,128)}, /*index=5*/s32[]{:T(128)}, s32[]{:T(128)}, s32[]{:T(128)}, s32[]{:T(128)}) while((s32[]{:T(128)}, f32[64,256]{1,0:T(8,128)S(1)}, f32[256]{0:T(256)S(1)}, ...), condition=%wide.region_3.0_spmd.clone, body=%wide.region_1.0_spmd.clone.sunk | while | flops 69239048 | bytes 1495198 | solution.py:58
  141.2 7.8 %fusion.22 = bf16[2,32,256,256]{2,3,0,1:T(8,128)(2,1)} fusion(bf16[256,32,128]{2,0,1:T(8,128)(2,1)} %collective-permute-done, bf16[1,256,32,128]{3,1,0,2:T(8,128)(2,1)} %copy-done, bf16[1,256,32,128]{3,1,0,2:T(8,128)(2,1)S(1)} %fusion.46), kind=kOutput, calls=%fused_computation.32 | convolution fusion | flops 1090519040 | bytes 14680064 | tf_op jit(solution)/shard_map/rifs,jfs->rfij/dot_general | solution.py:34
  149.0 11.9 %copy.18 = bf16[2,32,256,256]{3,2,1,0:T(8,128)(2,1)} copy(bf16[2,32,256,256]{2,3,0,1:T(8,128)(2,1)} %fusion.22) | data formatting | bytes 16777216 | tf_op jit(solution)/shard_map/convert_element_type | solution.py:35
  160.9 64.1 %while.48 = (s32[]{:T(128)}, f32[64,256]{1,0:T(8,128)S(1)}, f32[256]{0:T(256)S(1)}, bf16[64,256,256]{2,1,0:T(8,128)(2,1)}, s32[256,256]{1,0:T(8,128)S(1)}, /*index=5*/s32[]{:T(128)}, s32[]{:T(128)}, s32[]{:T(128)}, s32[]{:T(128)}) while((s32[]{:T(128)}, f32[64,256]{1,0:T(8,128)S(1)}, f32[256]{0:T(256)S(1)}, ...), condition=%wide.region_6.0_spmd.clone, body=%wide.region_4.0_spmd.clone.sunk | while | flops 69222408 | bytes 1495187 | solution.py:58
  170.9 1.0 constant_dynamic-slice_fusion.6
  174.9 1.0 constant_dynamic-slice_fusion.6
  179.0 1.0 constant_dynamic-slice_fusion.6
  209.0 1.0 constant_dynamic-slice_fusion.6
  225.0 7.8 %fusion.23 = bf16[2,32,256,256]{2,3,0,1:T(8,128)(2,1)} fusion(bf16[256,32,128]{2,0,1:T(8,128)(2,1)} %collective-permute-done.1, bf16[1,256,32,128]{3,1,0,2:T(8,128)(2,1)} %copy-done, bf16[1,256,32,128]{3,1,0,2:T(8,128)(2,1)S(1)} %fusion.46), kind=kOutput, calls=%fused_computation.33 | convolution fusion | flops 1090519040 | bytes 14680064 | tf_op jit(solution)/shard_map/rifs,jfs->rfij/dot_general | solution.py:34
  232.8 11.9 %copy.19 = bf16[2,32,256,256]{3,2,1,0:T(8,128)(2,1)} copy(bf16[2,32,256,256]{2,3,0,1:T(8,128)(2,1)} %fusion.23) | data formatting | bytes 16777216 | tf_op jit(solution)/shard_map/convert_element_type | solution.py:35
  244.7 64.1 %while.49 = (s32[]{:T(128)}, f32[64,256]{1,0:T(8,128)S(1)}, f32[256]{0:T(256)S(1)}, bf16[64,256,256]{2,1,0:T(8,128)(2,1)}, s32[256,256]{1,0:T(8,128)S(1)}, /*index=5*/s32[]{:T(128)}, s32[]{:T(128)}, s32[]{:T(128)}, s32[]{:T(128)}) while((s32[]{:T(128)}, f32[64,256]{1,0:T(8,128)S(1)}, f32[256]{0:T(256)S(1)}, ...), condition=%wide.region_9.0_spmd.clone, body=%wide.region_7.0_spmd.clone.sunk | while | flops 69222408 | bytes 1495187 | solution.py:58
  308.8 1.0 fusion.29
  309.9 125.1 %psum.7 = f32[256]{0:T(256)S(1)} all-reduce(f32[256]{0:T(256)S(1)} %get-tuple-element.340), channel_id=1, replica_groups=mesh['chan'=64,'off'=4] {'chan'}, use_global_device_ids=true, to_apply=%region_11.12 | all-reduce | flops 256 | bytes 2048 | tf_op jit(solution)/shard_map/psum | solution.py:81
  436.2 109.9 %all-reduce.3.cloned.1.call-done = f32[256,128]{1,0:T(8,128)} async-done(((f32[256,128]{1,0:T(8,128)}), f32[256,128]{1,0:T(8,128)}) %all-reduce.3.cloned.1.call-update) | async-done | bytes 131088
  546.2 1.2 dynamic-slice_divide_fusion
  (688 shorter events, 208.1 us)
Async XLA Ops:
  6.5 3.1 copy-start.1
  6.5 539.6 %all-reduce.3.cloned.1.call-start = ((), (), s32[]{:S(2)}) async-start(), calls=%async_computation | async-start | bytes 262144
  13.1 15.4 %copy-start.2 = (bf16[256,32,128]{2,1,0:T(8,128)(2,1)S(1)}, bf16[256,32,128]{2,1,0:T(8,128)(2,1)}, u32[]{:S(2)}) copy-start(bf16[256,32,128]{2,1,0:T(8,128)(2,1)} %param.8) | copy-start | bytes 6291460
  13.1 128.1 %collective-permute-start = (bf16[256,32,128]{2,0,1:T(8,128)(2,1)}, bf16[256,32,128]{2,0,1:T(8,128)(2,1)}, u32[]{:S(2)}, u32[]{:S(2)}) collective-permute-start(bf16[256,32,128]{2,0,1:T(8,128)(2,1)} %fusion.25), channel_id=1, source_target_pairs={{0,252},{4,0},{8,4},{12,8},{16,12},{20,16},{24,20},{28,24},{32,28}... | collective-permute-start | bytes 6291464 | tf_op jit(solution)/shard_map/ppermute | solution.py:14
  22.9 202.1 %collective-permute-start.1 = (bf16[256,32,128]{2,0,1:T(8,128)(2,1)}, bf16[256,32,128]{2,0,1:T(8,128)(2,1)}, u32[]{:S(2)}, u32[]{:S(2)}) collective-permute-start(bf16[256,32,128]{2,0,1:T(8,128)(2,1)} %fusion.25), channel_id=1, source_target_pairs={{0,248},{4,252},{8,0},{12,4},{16,8},{20,12},{24,16},{28,20},{32,24... | collective-permute-start | bytes 6291464 | tf_op jit(solution)/shard_map/ppermute | solution.py:14
  34.5 1.3 copy-start
  42.0 12.0 %copy-start.3 = (s32[1,3,256,256]{3,2,1,0:T(8,128)S(1)}, s32[1,3,256,256]{3,2,1,0:T(8,128)}, u32[]{:S(2)}) copy-start(s32[1,3,256,256]{3,2,1,0:T(8,128)} %param.9) | copy-start | bytes 2359300
Sparse Core Ops, SparseCore 0:
  310.0 236.1 all-reduce.2
where the time goes:
time: 560 us; the launch traced here: 554 us
  local copies, waits for them, and re-layouts  161 us (29%)
  blocking collectives  125 us (22%)
  waiting for transfers between devices  110 us (20%)
  matrix products  75.6 us (13%)
  other arithmetic  53.6 us (10%)
  between operations  14.2 us (3%)
  starting transfers between devices  10.5 us (2%)
    psum x1, blocking collectives, on_device(): all_counts = lax.psum(counts, 'chan')  125 us
    unnamed x2, waiting for transfers between devices  110 us
    dynamic_slice x96, local copies, waits for them, and re-layouts, add_block(): lax.dynamic_slice_in_dim(cross, block_index * rows, rows, 1)  93.4 us
    dot_general x96, matrix products, add_block(): jnp.dot(piece, onehot.astype(jnp.bfloat16), preferred_element_type=jnp.fl...  52.8 us
    convert_element_type x3, local copies, waits for them, and re-layouts, cross_pairs(): cross = (cross * (1.0 / half)).astype(jnp.bfloat16)  35.8 us
    reduce_sum x96, other arithmetic, add_block(): tallies = tallies + jnp.sum(onehot.astype(jnp.float32), axis=0)  33.7 us
    while x288, local copies, waits for them, and re-layouts  28.7 us
    dot_general x3, matrix products, cross_pairs(): jnp.einsum('rifs,jfs->rfij', both, other, preferred_element_type=jnp.floa...  21.7 us
  transfers between devices with their start and end apart: 3, of which 1 were waited for; matrix products, arithmetic and copies ran while one was open for 36% of the time, Pallas kernels for 0%

commit v1 on v0

v1 whole, which is shorter than its diff:
```python
import functools
import math

import jax
import jax.numpy as jnp
from jax import lax
from jax.experimental import pallas as pl
from jax.experimental.pallas import tpu as pltpu
from jax.sharding import PartitionSpec as P

F32 = jnp.float32
BF16 = jnp.bfloat16
MESH = pl.DeviceIdType.MESH
VMEM = pl.BlockSpec(memory_space=pltpu.VMEM)

CH = 256
LANES = 128
HALF = LANES // 2
SEGMENTS = 4
CLASSES = 64
PAD = 8
NEAR = 8
FAR = 32
FREQ_UNROLL = 8
ROW_UNROLL = 32


def whiten(raw, rows, white, with_rotated):
    freqs = raw.shape[1]
    step = freqs + PAD
    chunk = 32

    def normalise(block, _):
        values = raw[pl.ds(block * chunk, chunk)].astype(F32)
        meansq = jnp.mean(values * values, axis=-1, keepdims=True)
        scaled = values * lax.rsqrt(meansq + 1e-05)
        for channel in range(chunk):
            start = pl.multiple_of((block * chunk + channel) * step, 8)
            rows[pl.ds(start, freqs), :] = scaled[channel]
        return 0

    lax.fori_loop(0, CH // chunk, normalise, 0)

    def regroup(block, _):
        for part in range(FREQ_UNROLL):
            freq = block * FREQ_UNROLL + part
            values = rows[pl.ds(freq, CH, stride=step), :]
            white[freq, :CH, :] = values.astype(BF16)
            if with_rotated:
                lane = lax.broadcasted_iota(jnp.int32, (CH, LANES), 1)
                turned = pltpu.roll(values, HALF, 1)
                white[freq, CH:, :] = jnp.where(lane < HALF, turned, -turned).astype(BF16)
        return 0

    lax.fori_loop(0, freqs // FREQ_UNROLL, regroup, 0)


def cross_pairs(own, other, cross):
    freqs = other.shape[0]
    step = CH + PAD

    def body(block, _):
        for part in range(FREQ_UNROLL):
            freq = block * FREQ_UNROLL + part
            product = lax.dot_general(
                own[freq], other[freq], (((1,), (1,)), ((), ())), preferred_element_type=F32
            )
            for row in range(2):
                start = pl.multiple_of((freq + row * freqs) * step, 8)
                for side in range(2):
                    cross[side, pl.ds(start, CH), :] = product[
                        row * CH : (row + 1) * CH, side * LANES : (side + 1) * LANES
                    ]
        return 0

    lax.fori_loop(0, freqs // FREQ_UNROLL, body, 0)


def add_bins(cross, labels, slots, sums, counts):
    step = CH + PAD
    nrows = sums.shape[1]
    shape = (CLASSES // 16, 16, CH)
    slot_ids = lax.broadcasted_iota(jnp.int32, shape, 0) * 16 + lax.broadcasted_iota(jnp.int32, shape, 1)
    slot_ids = slot_ids.astype(F32).astype(BF16)
    one = jnp.ones((), BF16)
    zero = jnp.zeros((), BF16)
    segments = labels[...] & (SEGMENTS - 1)
    first, last = jnp.min(segments), jnp.max(segments)

    def add_segment(segment, _):
        marks = labels[...]
        classes = lax.shift_right_logical(marks, 2)
        slot = (classes & 1) * (CLASSES // 2) + lax.shift_right_logical(classes, 1)
        slots[...] = jnp.where((marks & (SEGMENTS - 1)) == segment, slot.astype(F32), -1.0)

        def add_rows(block, _):
            pieces, onehots = [], []
            tally = None
            for part in range(ROW_UNROLL):
                i = block * ROW_UNROLL + part
                sides = [cross[side, pl.ds(i, nrows, stride=step), :] for side in range(2)]
                pieces.append(jnp.concatenate(sides, axis=1).astype(BF16))
                row = jnp.broadcast_to(slots[pl.ds(i, 1), :], (16, CH)).astype(BF16)
                onehot = jnp.where(row[None] == slot_ids, one, zero).reshape(CLASSES, CH)
                onehots.append(onehot)
                tally = onehot if tally is None else tally + onehot
            sums[segment] += lax.dot_general(
                jnp.concatenate(pieces, axis=1),
                jnp.concatenate(onehots, axis=1),
                (((1,), (1,)), ((), ())),
                preferred_element_type=F32,
            )
            counts[segment] += tally.astype(F32)
            return 0

        lax.fori_loop(0, CH // ROW_UNROLL, add_rows, 0)
        return 0

    lax.fori_loop(first, last + 1, add_segment, 0)


def self_kernel(raw, labels, white, sums, counts, rows, cross, slots):
    sums[...] = jnp.zeros_like(sums)
    counts[...] = jnp.zeros_like(counts)
    whiten(raw, rows, white, True)
    cross_pairs(white, white.at[:, :CH, :], cross)
    add_bins(cross, labels, slots, sums, counts)


def pair_kernel(white, raw, labels, sums_in, counts_in, sums, counts, rows, other, cross, slots):
    sums[...] = sums_in[...]
    counts[...] = counts_in[...]
    whiten(raw, rows, other, False)
    cross_pairs(white, other, cross)
    add_bins(cross, labels, slots, sums, counts)


def last_kernel(
    white, raw, labels, sums_in, counts_in, table, share, parts, sums, counts, rows, other, cross, slots
):
    pair_kernel(white, raw, labels, sums_in, counts_in, sums, counts, rows, other, cross, slots)
    for segment in range(SEGMENTS):
        trace = lax.dot_general(
            sums[segment],
            table[...],
            (((0,), (0,)), ((), ())),
            precision=lax.Precision.HIGHEST,
            preferred_element_type=F32,
        )
        tally = jnp.sum(counts[segment], axis=1, keepdims=True) * share[0:1, :]
        for low in range(2):
            part = slice(low * FAR, (low + 1) * FAR)
            parts[segment * 2 + low, :, :LANES] = trace[part]
            parts[segment * 2 + low, :, LANES:] = tally[part]


def reduce_kernel(parts, out, near_in, far_out, far_in, near_send, near_recv, far_send, far_recv):
    chan, off = lax.axis_index("chan"), lax.axis_index("off")
    low, high = lax.rem(chan, 2), lax.div(chan, 2)
    near = off * 2 + low

    def near_device(step):
        index = lax.rem(near + step, NEAR)
        return index, (high * 2 + lax.rem(index, 2), lax.div(index, 2))

    def far_device(step):
        index = lax.rem(high + step, FAR)
        return index, (index * 2 + low, off)

    barrier = pltpu.get_barrier_semaphore()

    def greet_near(step, _):
        pl.semaphore_signal(barrier, inc=1, device_id=near_device(step)[1], device_id_type=MESH)
        return 0

    def greet_far(step, _):
        pl.semaphore_signal(barrier, inc=1, device_id=far_device(step)[1], device_id_type=MESH)
        return 0

    lax.fori_loop(1, FAR, greet_far, 0)
    lax.fori_loop(1, NEAR, greet_near, 0)
    pl.semaphore_wait(barrier, FAR - 1 + NEAR - 1)

    def near_copy(step):
        index, device = near_device(step)
        return pltpu.make_async_remote_copy(
            src_ref=parts.at[index],
            dst_ref=near_in.at[step - 1],
            send_sem=near_send.at[step - 1],
            recv_sem=near_recv.at[step - 1],
            device_id=device,
            device_id_type=MESH,
        )

    def far_copy(step):
        index, device = far_device(step)
        return pltpu.make_async_remote_copy(
            src_ref=far_out.at[index],
            dst_ref=far_in.at[step - 1],
            send_sem=far_send.at[step - 1],
            recv_sem=far_recv.at[step - 1],
            device_id=device,
            device_id_type=MESH,
        )

    def start_near(step, _):
        near_copy(step).start()
        return 0

    def start_far(step, _):
        far_copy(step).start()
        return 0

    lax.fori_loop(1, NEAR, start_near, 0)

    def add_near(step, total):
        near_copy(step).wait_recv()
        return total + near_in[step - 1]

    total = lax.fori_loop(1, NEAR, add_near, parts[near])
    for row in range(FAR):
        far_out[row] = total[row : row + 1]
    lax.fori_loop(1, FAR, start_far, 0)

    def add_far(step, total):
        far_copy(step).wait_recv()
        return total + far_in[step - 1]

    total = lax.fori_loop(1, FAR, add_far, far_out[high])
    out[...] = total[:, :LANES] / jnp.sqrt(jnp.maximum(total[:, LANES:], 1.0))

    def end_near(step, _):
        near_copy(step).wait_send()
        return 0

    def end_far(step, _):
        far_copy(step).wait_send()
        return 0

    lax.fori_loop(1, NEAR, end_near, 0)
    lax.fori_loop(1, FAR, end_far, 0)


def lag_table(freqs, nfreq, lags):
    shifts = jnp.arange(lags, dtype=jnp.int32) - lags // 2
    phase = jnp.mod(freqs[:, None] * shifts[None, :], 2 * nfreq)
    theta = math.pi * phase.astype(F32) / nfreq
    return jnp.concatenate([jnp.cos(theta), -jnp.sin(theta)], axis=0)


def from_ahead(value, steps):
    count = lax.axis_size("chan")
    pairs = [(source, (source - steps) % count) for source in range(count)]
    return lax.ppermute(value, "chan", pairs)


def on_device(spectra, pair_bins):
    freqs = spectra.shape[1]
    params = pltpu.CompilerParams(vmem_limit_bytes=48 * 1024 * 1024)
    rows = pltpu.VMEM((CH * (freqs + PAD), LANES), F32)
    other = pltpu.VMEM((freqs, CH, LANES), BF16)
    cross = pltpu.VMEM((2, 2 * freqs * (CH + PAD), LANES), F32)
    slots = pltpu.VMEM((CH, CH), F32)
    white_shape = jax.ShapeDtypeStruct((freqs, 2 * CH, LANES), BF16)
    sums_shape = jax.ShapeDtypeStruct((SEGMENTS, 2 * freqs, CLASSES), F32)
    counts_shape = jax.ShapeDtypeStruct((SEGMENTS, CLASSES, CH), F32)
    parts_shape = jax.ShapeDtypeStruct((NEAR, FAR, 2 * LANES), F32)

    ahead = [from_ahead(spectra, step) for step in (1, 2)]
    labels = pair_bins[0]
    nfreq = freqs * lax.axis_size("off")
    own_freqs = lax.axis_index("off") * freqs + jnp.arange(freqs, dtype=jnp.int32)
    table = lag_table(own_freqs, nfreq, LANES) * (1.0 / HALF)
    share = jnp.full((8, LANES), lax.axis_index("off") == 0, F32)

    white, sums, counts = pl.pallas_call(
        self_kernel,
        out_shape=[white_shape, sums_shape, counts_shape],
        in_specs=[VMEM] * 2,
        out_specs=[VMEM] * 3,
        scratch_shapes=[rows, cross, slots],
        compiler_params=params,
        cost_estimate=pl.CostEstimate(flops=3 * 10**9, bytes_accessed=10**7, transcendentals=0),
    )(spectra, labels[0])
    sums, counts = pl.pallas_call(
        pair_kernel,
        out_shape=[sums_shape, counts_shape],
        in_specs=[VMEM] * 5,
        out_specs=[VMEM] * 2,
        scratch_shapes=[rows, other, cross, slots],
        compiler_params=params,
        cost_estimate=pl.CostEstimate(flops=3 * 10**9, bytes_accessed=10**7, transcendentals=0),
    )(white, ahead[0], labels[1], sums, counts)
    parts = pl.pallas_call(
        last_kernel,
        out_shape=parts_shape,
        in_specs=[VMEM] * 7,
        out_specs=VMEM,
        scratch_shapes=[
            pltpu.VMEM(sums_shape.shape, F32),
            pltpu.VMEM(counts_shape.shape, F32),
            rows,
            other,
            cross,
            slots,
        ],
        compiler_params=params,
        cost_estimate=pl.CostEstimate(flops=3 * 10**9, bytes_accessed=10**7, transcendentals=0),
    )(white, ahead[1], labels[2], sums, counts, table, share)
    return pl.pallas_call(
        reduce_kernel,
        out_shape=jax.ShapeDtypeStruct((1, LANES), F32),
        in_specs=[VMEM],
        out_specs=VMEM,
        scratch_shapes=[
            pltpu.VMEM((NEAR - 1, FAR, 2 * LANES), F32),
            pltpu.VMEM((FAR, 1, 2 * LANES), F32),
            pltpu.VMEM((FAR - 1, 1, 2 * LANES), F32),
            pltpu.SemaphoreType.DMA((NEAR - 1,)),
            pltpu.SemaphoreType.DMA((NEAR - 1,)),
            pltpu.SemaphoreType.DMA((FAR - 1,)),
            pltpu.SemaphoreType.DMA((FAR - 1,)),
        ],
        compiler_params=pltpu.CompilerParams(collective_id=0, has_side_effects=True),
    )(parts)


def solution(mesh):
    in_specs = (P("chan", "off", None), P("chan", None, None, None))
    out_specs = P(("chan", "off"), None)
    return jax.shard_map(
        on_device, mesh=mesh, in_specs=in_specs, out_specs=out_specs, check_vma=False
    )
```

time: 560 us -> 176 us (0.31)
  local copies, waits for them, and re-layouts: 161 us -> 4.62 us
  blocking collectives: 125 us -> 0 us
  matrix products: 75.6 us -> 0 us
  Pallas kernels: 0 us -> 57.5 us
  other arithmetic: 53.6 us -> 0.17 us
  between operations: 14.2 us -> 0.05 us
  waiting for transfers between devices: 110 us -> 103 us
    psum x1 -> x0, blocking collectives: 125 us -> none  [on_device(): all_counts = lax.psum(counts, 'chan')]
    unnamed x2 -> x0, waiting for transfers between devices: 110 us -> none
    ppermute x2, waiting for transfers between devices: 0.01 us -> 103 us  [from_ahead(): return lax.ppermute(value, 'chan', pairs)]
    dynamic_slice x97 -> x0, local copies, waits for them, and re-layouts: 93.9 us -> none  [the longest x96 93.4 us: add_block(): lax.dynamic_slice_in_dim(cross, block_index * rows, rows, 1)]
    dot_general x100 -> x0, matrix products: 75.6 us -> none  [the longest x96 52.8 us: add_block(): jnp.dot(piece, onehot.astype(jnp.bfloat16), preferred_element_type=jnp.fl...]
    pallas_call x0 -> x4, Pallas kernels: none -> 57.5 us  [the longest x1 20.2 us: on_device(): pl.pallas_call(reduce_kernel, out_shape=jax.ShapeDtypeStruct((1, LANES),...]
    reduce_sum x97 -> x0, other arithmetic: 36.7 us -> none  [the longest x96 33.7 us: add_block(): tallies = tallies + jnp.sum(onehot.astype(jnp.float32), axis=0)]
    convert_element_type x3 -> x0, local copies, waits for them, and re-layouts: 35.8 us -> none  [cross_pairs(): cross = (cross * (1.0 / half)).astype(jnp.bfloat16)]
  transfers between devices with their start and end apart: 3 -> 2, of which waited for: 1 -> 2; matrix products, arithmetic and copies ran while one was open for 36% -> 1% of each run, Pallas kernels for 0% -> 14%
where the time goes in v1:
time: 176 us; the launch traced here: 175 us
  waiting for transfers between devices  103 us (59%)
  Pallas kernels  57.5 us (33%)
  starting transfers between devices  10.5 us (6%)
  local copies, waits for them, and re-layouts  4.62 us (3%)
    ppermute x2, waiting for transfers between devices, from_ahead(): return lax.ppermute(value, 'chan', pairs)  103 us
    pallas_call x1, Pallas kernels, on_device(): pl.pallas_call(reduce_kernel, out_shape=jax.ShapeDtypeStruct((1, LANES),...  20.2 us
    pallas_call x1, Pallas kernels, on_device(): pl.pallas_call(pair_kernel, out_shape=[sums_shape, counts_shape], in_spec...  12.6 us
    pallas_call x1, Pallas kernels, on_device(): pl.pallas_call(self_kernel, out_shape=[white_shape, sums_shape, counts_sh...  12.5 us
    pallas_call x1, Pallas kernels, on_device(): pl.pallas_call(last_kernel, out_shape=parts_shape, in_specs=[VMEM] * 7, o...  12.2 us
    ppermute x2, starting transfers between devices, from_ahead(): return lax.ppermute(value, 'chan', pairs)  10.5 us
  transfers between devices with their start and end apart: 2, of which 2 were waited for; matrix products, arithmetic and copies ran while one was open for 1% of the time, Pallas kernels for 14%

profile of v1, /device:TPU:1, one launch (start us, length us, event | category | flops | bytes accessed | tf_op | source)
XLA Modules:
  0.0 175.4 jit_solution(10272588894671050133)
XLA Ops:
  0.0 9.8 %collective-permute-start.1 = (bf16[256,32,128]{2,1,0:T(8,128)(2,1)}, bf16[256,32,128]{2,1,0:T(8,128)(2,1)}, u32[]{:S(2)}, u32[]{:S(2)}) collective-permute-start(bf16[256,32,128]{2,1,0:T(8,128)(2,1)} %raw.1), channel_id=1, source_target_pairs={{0,252},{4,0},{8,4},{12,8},{16,12},{20,16},{24,20},{28,24},{32,28}... | collective-permute-start | bytes 6291464 | tf_op jit(solution)/shard_map/ppermute | solution.py:254
  9.8 0.7 collective-permute-start
  10.5 0.2 fusion.3
  10.7 1.2 slice_bitcast_fusion
  11.9 0.0 copy-start.1
  11.9 1.6 copy-done.1
  13.5 12.5 %shard_map.28 = (bf16[32,512,128]{2,1,0:T(8,128)(2,1)}, f32[4,64,64]{2,1,0:T(8,128)S(1)}, f32[4,64,256]{2,1,0:T(8,128)S(1)}) custom-call(bf16[256,32,128]{2,1,0:T(8,128)(2,1)S(1)} %copy-done.1, s32[256,256]{1,0:T(8,128)S(1)} %get-tuple-element.16.labels), custom_call_target="tpu_custom_call" | custom-call | flops 3000000000 | bytes 10000000 | tf_op jit(solution)/shard_map/pallas_call | solution.py:276
  25.9 70.2 %collective-permute-done.1.raw = bf16[256,32,128]{2,1,0:T(8,128)(2,1)} collective-permute-done((bf16[256,32,128]{2,1,0:T(8,128)(2,1)}, bf16[256,32,128]{2,1,0:T(8,128)(2,1)}, u32[]{:S(2)}, u32[]{:S(2)}) %collective-permute-start.1) | collective-permute-done | bytes 2097184 | tf_op jit(solution)/shard_map/ppermute | solution.py:254
  96.1 12.6 %shard_map.29 = (f32[4,64,64]{2,1,0:T(8,128)S(1)}, f32[4,64,256]{2,1,0:T(8,128)S(1)}) custom-call(bf16[32,512,128]{2,1,0:T(8,128)(2,1)} %get-tuple-element.10.white, bf16[256,32,128]{2,1,0:T(8,128)(2,1)} %collective-permute-done.1.raw, s32[256,256]{1,0:T(8,128)S(1)} %get-tuple-element.15.labels, f32[4,64,64]{2,1,0:T(8,128)S(1)} %get-tuple-element.11.sums_in, ...), custom_call_target="tpu_custom_call" | custom-call | flops 3000000000 | bytes 10000000 | tf_op jit(solution)/shard_map/pallas_call | solution.py:285
  108.7 32.4 %collective-permute-done.raw = bf16[256,32,128]{2,1,0:T(8,128)(2,1)S(1)} collective-permute-done((bf16[256,32,128]{2,1,0:T(8,128)(2,1)}, bf16[256,32,128]{2,1,0:T(8,128)(2,1)S(1)}, u32[]{:S(2)}, u32[]{:S(2)}) %collective-permute-start) | collective-permute-done | bytes 2097184 | tf_op jit(solution)/shard_map/ppermute | solution.py:254
  141.1 12.2 %shard_map.30.parts = f32[8,32,256]{2,1,0:T(8,128)S(1)} custom-call(bf16[32,512,128]{2,1,0:T(8,128)(2,1)} %get-tuple-element.10.white, bf16[256,32,128]{2,1,0:T(8,128)(2,1)S(1)} %collective-permute-done.raw, s32[256,256]{1,0:T(8,128)S(1)} %get-tuple-element.17.labels, f32[4,64,64]{2,1,0:T(8,128)S(1)} %get-tuple-element.13.sums_in, ...), custom_call_target="tpu_custom_call" | custom-call | flops 3000000000 | bytes 10000000 | tf_op jit(solution)/shard_map/pallas_call | solution.py:294
  153.4 0.0 copy-start
  153.4 0.7 copy-done
  154.1 20.2 %shard_map.31 = f32[1,128]{1,0:T(1,128)} custom-call(f32[8,32,256]{2,1,0:T(8,128)} %copy-done), custom_call_target="tpu_custom_call" | custom-call | tf_op jit(solution)/shard_map/pallas_call | solution.py:310
  174.2 1.2 copy.4
  (4 shorter events, 0.0 us)
Async XLA Ops:
  0.0 96.1 %collective-permute-start.1 = (bf16[256,32,128]{2,1,0:T(8,128)(2,1)}, bf16[256,32,128]{2,1,0:T(8,128)(2,1)}, u32[]{:S(2)}, u32[]{:S(2)}) collective-permute-start(bf16[256,32,128]{2,1,0:T(8,128)(2,1)} %raw.1), channel_id=1, source_target_pairs={{0,252},{4,0},{8,4},{12,8},{16,12},{20,16},{24,20},{28,24},{32,28}... | collective-permute-start | bytes 6291464 | tf_op jit(solution)/shard_map/ppermute | solution.py:254
  9.8 131.3 %collective-permute-start = (bf16[256,32,128]{2,1,0:T(8,128)(2,1)}, bf16[256,32,128]{2,1,0:T(8,128)(2,1)S(1)}, u32[]{:S(2)}, u32[]{:S(2)}) collective-permute-start(bf16[256,32,128]{2,1,0:T(8,128)(2,1)} %raw.1), channel_id=1, source_target_pairs={{0,248},{4,252},{8,0},{12,4},{16,8},{20,12},{24,16},{28,20},{32,24... | collective-permute-start | bytes 6291464 | tf_op jit(solution)/shard_map/ppermute | solution.py:254
  11.9 1.6 copy-start.1
  153.4 0.7 copy-start

commit v2 on v1

--- a/solution.py
+++ b/solution.py
@@ -55,18 +55,18 @@
     lax.fori_loop(0, freqs // FREQ_UNROLL, regroup, 0)
 
 
-def cross_pairs(own, other, cross):
-    freqs = other.shape[0]
+def cross_pairs(first, second, cross, top):
+    freqs = second.shape[0]
     step = CH + PAD
 
     def body(block, _):
         for part in range(FREQ_UNROLL):
             freq = block * FREQ_UNROLL + part
             product = lax.dot_general(
-                own[freq], other[freq], (((1,), (1,)), ((), ())), preferred_element_type=F32
+                first[freq], second[freq, :CH, :], (((1,), (1,)), ((), ())), preferred_element_type=F32
             )
             for row in range(2):
-                start = pl.multiple_of((freq + row * freqs) * step, 8)
+                start = pl.multiple_of((top + freq + row * freqs) * step, 8)
                 for side in range(2):
                     cross[side, pl.ds(start, CH), :] = product[
                         row * CH : (row + 1) * CH, side * LANES : (side + 1) * LANES
@@ -76,19 +76,18 @@
     lax.fori_loop(0, freqs // FREQ_UNROLL, body, 0)
 
 
-def add_bins(cross, labels, slots, sums, counts):
+def add_bins(cross, read_labels, weight, slots, nrows, add_sums, counts):
     step = CH + PAD
-    nrows = sums.shape[1]
     shape = (CLASSES // 16, 16, CH)
     slot_ids = lax.broadcasted_iota(jnp.int32, shape, 0) * 16 + lax.broadcasted_iota(jnp.int32, shape, 1)
     slot_ids = slot_ids.astype(F32).astype(BF16)
     one = jnp.ones((), BF16)
     zero = jnp.zeros((), BF16)
-    segments = labels[...] & (SEGMENTS - 1)
+    segments = read_labels() & (SEGMENTS - 1)
     first, last = jnp.min(segments), jnp.max(segments)
 
     def add_segment(segment, _):
-        marks = labels[...]
+        marks = read_labels()
         classes = lax.shift_right_logical(marks, 2)
         slot = (classes & 1) * (CLASSES // 2) + lax.shift_right_logical(classes, 1)
         slots[...] = jnp.where((marks & (SEGMENTS - 1)) == segment, slot.astype(F32), -1.0)
@@ -104,13 +103,16 @@
                 onehot = jnp.where(row[None] == slot_ids, one, zero).reshape(CLASSES, CH)
                 onehots.append(onehot)
                 tally = onehot if tally is None else tally + onehot
-            sums[segment] += lax.dot_general(
-                jnp.concatenate(pieces, axis=1),
-                jnp.concatenate(onehots, axis=1),
-                (((1,), (1,)), ((), ())),
-                preferred_element_type=F32,
+            add_sums(
+                segment,
+                lax.dot_general(
+                    jnp.concatenate(pieces, axis=1),
+                    jnp.concatenate(onehots, axis=1),
+                    (((1,), (1,)), ((), ())),
+                    preferred_element_type=F32,
+                ),
             )
-            counts[segment] += tally.astype(F32)
+            counts[segment] += tally.astype(F32) * weight
             return 0
 
         lax.fori_loop(0, CH // ROW_UNROLL, add_rows, 0)
@@ -122,36 +124,74 @@
 def self_kernel(raw, labels, white, sums, counts, rows, cross, slots):
     sums[...] = jnp.zeros_like(sums)
     counts[...] = jnp.zeros_like(counts)
-    whiten(raw, rows, white, True)
-    cross_pairs(white, white.at[:, :CH, :], cross)
-    add_bins(cross, labels, slots, sums, counts)
-
-
-def pair_kernel(white, raw, labels, sums_in, counts_in, sums, counts, rows, other, cross, slots):
+    half = white.shape[1]
+    whiten(raw, rows, white.reshape(2 * half, 2 * CH, LANES), True)
+    for side in range(2):
+        cross_pairs(white.at[side], white.at[side], cross, side * 2 * half)
+
+    def add_sums(segment, values):
+        for side in range(2):
+            sums[segment, side] += values[side * 2 * half : (side + 1) * 2 * half]
+
+    weight = (lax.axis_index("off") == 0).astype(F32)
+    add_bins(cross, lambda: labels[...], weight, slots, 4 * half, add_sums, counts)
+
+
+def pairs_kernel(
+    own, beside, after, before, labels, labels_beside, labels_before, sums_in, counts_in, table,
+    parts, sums, counts, white, rows, cross, slots, own_sem,
+):
+    half = own.shape[1]
+    copy = pltpu.make_async_copy(own, white.at[0:2], own_sem)
+    copy.start()
     sums[...] = sums_in[...]
     counts[...] = counts_in[...]
-    whiten(raw, rows, other, False)
-    cross_pairs(white, other, cross)
-    add_bins(cross, labels, slots, sums, counts)
-
-
-def last_kernel(
-    white, raw, labels, sums_in, counts_in, table, share, parts, sums, counts, rows, other, cross, slots
-):
-    pair_kernel(white, raw, labels, sums_in, counts_in, sums, counts, rows, other, cross, slots)
+    whiten(beside, rows, white.at[2], True)
+    whiten(after, rows, white.at[3], False)
+    whiten(before, rows, white.at[4], True)
+    copy.wait()
+    low = lax.rem(lax.axis_index("chan"), 2)
+    counted = (lax.axis_index("off") == 0).astype(F32)
+    even = (1 - low).astype(F32) * counted
+    odd = low.astype(F32) * counted
+
+    def moved(ref):
+        return ref[...].astype(F32).astype(jnp.int32)
+
+    def choose(if_even, if_odd):
+        return lambda: jnp.where(low == 0, if_even(), if_odd())
+
+    own_near, own_far = lambda: labels[1], lambda: labels[2]
+    beside_near = lambda: moved(labels_beside)
+    before_near, before_far = lambda: moved(labels_before.at[0]), lambda: moved(labels_before.at[1])
+    jobs = (
+        ((0, 2), (2, 1), choose(own_near, beside_near), low, even),
+        ((0, 3), (4, 1), choose(own_far, before_far), low, even),
+        ((2, 3), (4, 2), choose(beside_near, before_near), low, even),
+        ((4, 1), (0, 3), choose(before_far, own_far), 1 - low, odd),
+    )
+    for if_even, if_odd, read_labels, side, weight in jobs:
+        first = if_even[0] + low * (if_odd[0] - if_even[0])
+        second = if_even[1] + low * (if_odd[1] - if_even[1])
+        cross_pairs(white.at[first], white.at[second], cross, 0)
+
+        def add_sums(segment, values):
+            sums[segment, side] += values
+
+        add_bins(cross, read_labels, weight, slots, 2 * half, add_sums, counts)
     for segment in range(SEGMENTS):
         trace = lax.dot_general(
-            sums[segment],
+            sums[segment].reshape(4 * half, CLASSES),
             table[...],
             (((0,), (0,)), ((), ())),
             precision=lax.Precision.HIGHEST,
             preferred_element_type=F32,
         )
-        tally = jnp.sum(counts[segment], axis=1, keepdims=True) * share[0:1, :]
-        for low in range(2):
-            part = slice(low * FAR, (low + 1) * FAR)
-            parts[segment * 2 + low, :, :LANES] = trace[part]
-            parts[segment * 2 + low, :, LANES:] = tally[part]
+        tally = jnp.sum(counts[segment], axis=1, keepdims=True)
+        for part in range(2):
+            piece = slice(part * FAR, (part + 1) * FAR)
+            parts[segment * 2 + part, :, :LANES] = trace[piece]
+            parts[segment * 2 + part, :, LANES:] = jnp.broadcast_to(tally[piece], (FAR, LANES))
 
 
 def reduce_kernel(parts, out, near_in, far_out, far_in, near_send, near_recv, far_send, far_recv):
@@ -245,68 +285,72 @@
     shifts = jnp.arange(lags, dtype=jnp.int32) - lags // 2
     phase = jnp.mod(freqs[:, None] * shifts[None, :], 2 * nfreq)
     theta = math.pi * phase.astype(F32) / nfreq
-    return jnp.concatenate([jnp.cos(theta), -jnp.sin(theta)], axis=0)
-
-
-def from_ahead(value, steps):
+    return jnp.stack([jnp.cos(theta), -jnp.sin(theta)], axis=0)
+
+
+def shifted(value, steps):
     count = lax.axis_size("chan")
-    pairs = [(source, (source - steps) % count) for source in range(count)]
-    return lax.ppermute(value, "chan", pairs)
+    return lax.ppermute(value, "chan", [(place, (place + steps) % count) for place in range(count)])
+
+
+def swapped(value):
+    count = lax.axis_size("chan")
+    return lax.ppermute(value, "chan", [(place, place ^ 1) for place in range(count)])
 
 
 def on_device(spectra, pair_bins):
     freqs = spectra.shape[1]
+    half = freqs // 2
+    low = lax.rem(lax.axis_index("chan"), 2)
     params = pltpu.CompilerParams(vmem_limit_bytes=48 * 1024 * 1024)
-    rows = pltpu.VMEM((CH * (freqs + PAD), LANES), F32)
-    other = pltpu.VMEM((freqs, CH, LANES), BF16)
-    cross = pltpu.VMEM((2, 2 * freqs * (CH + PAD), LANES), F32)
+    sums_shape = jax.ShapeDtypeStruct((SEGMENTS, 2, 2 * half, CLASSES), F32)
+    counts_shape = jax.ShapeDtypeStruct((SEGMENTS, CLASSES, CH), F32)
     slots = pltpu.VMEM((CH, CH), F32)
-    white_shape = jax.ShapeDtypeStruct((freqs, 2 * CH, LANES), BF16)
-    sums_shape = jax.ShapeDtypeStruct((SEGMENTS, 2 * freqs, CLASSES), F32)
-    counts_shape = jax.ShapeDtypeStruct((SEGMENTS, CLASSES, CH), F32)
-    parts_shape = jax.ShapeDtypeStruct((NEAR, FAR, 2 * LANES), F32)
-
-    ahead = [from_ahead(spectra, step) for step in (1, 2)]
+    cost = pl.CostEstimate(flops=3 * 10**9, bytes_accessed=10**7, transcendentals=0)
+
     labels = pair_bins[0]
+    after = shifted(spectra[:, :half], -2)
+    before = shifted(spectra[:, half:], 2)
+    beside = swapped(lax.dynamic_slice_in_dim(spectra, (1 - low) * half, half, 1))
+    sent_labels = labels[1:].astype(BF16)
+    labels_beside = swapped(sent_labels[0])
+    labels_before = shifted(sent_labels, 2)
+
     nfreq = freqs * lax.axis_size("off")
     own_freqs = lax.axis_index("off") * freqs + jnp.arange(freqs, dtype=jnp.int32)
     table = lag_table(own_freqs, nfreq, LANES) * (1.0 / HALF)
-    share = jnp.full((8, LANES), lax.axis_index("off") == 0, F32)
+    table = table.reshape(2, 2, half, LANES).swapaxes(0, 1).reshape(2 * freqs, LANES)
 
     white, sums, counts = pl.pallas_call(
         self_kernel,
-        out_shape=[white_shape, sums_shape, counts_shape],
+        out_shape=[jax.ShapeDtypeStruct((2, half, 2 * CH, LANES), BF16), sums_shape, counts_shape],
         in_specs=[VMEM] * 2,
         out_specs=[VMEM] * 3,
-        scratch_shapes=[rows, cross, slots],
+        scratch_shapes=[
+            pltpu.VMEM((CH * (freqs + PAD), LANES), F32),
+            pltpu.VMEM((2, 2 * freqs * (CH + PAD), LANES), F32),
+            slots,
+        ],
         compiler_params=params,
-        cost_estimate=pl.CostEstimate(flops=3 * 10**9, bytes_accessed=10**7, transcendentals=0),
+        cost_estimate=cost,
     )(spectra, labels[0])
-    sums, counts = pl.pallas_call(
-        pair_kernel,
-        out_shape=[sums_shape, counts_shape],
-        in_specs=[VMEM] * 5,
-        out_specs=[VMEM] * 2,
-        scratch_shapes=[rows, other, cross, slots],
-        compiler_params=params,
-        cost_estimate=pl.CostEstimate(flops=3 * 10**9, bytes_accessed=10**7, transcendentals=0),
-    )(white, ahead[0], labels[1], sums, counts)
     parts = pl.pallas_call(
-        last_kernel,
-        out_shape=parts_shape,
-        in_specs=[VMEM] * 7,
+        pairs_kernel,
+        out_shape=jax.ShapeDtypeStruct((NEAR, FAR, 2 * LANES), F32),
+        in_specs=[pl.BlockSpec(memory_space=pl.ANY)] + [VMEM] * 9,
         out_specs=VMEM,
         scratch_shapes=[
             pltpu.VMEM(sums_shape.shape, F32),
             pltpu.VMEM(counts_shape.shape, F32),
-            rows,
-            other,
-            cross,
+            pltpu.VMEM((5, half, 2 * CH, LANES), BF16),
+            pltpu.VMEM((CH * (half + PAD), LANES), F32),
+            pltpu.VMEM((2, 2 * half * (CH + PAD), LANES), F32),
             slots,
+            pltpu.SemaphoreType.DMA,
         ],
         compiler_params=params,
-        cost_estimate=pl.CostEstimate(flops=3 * 10**9, bytes_accessed=10**7, transcendentals=0),
-    )(white, ahead[1], labels[2], sums, counts, table, share)
+        cost_estimate=cost,
+    )(white, beside, after, before, labels, labels_beside, labels_before, sums, counts, table)
     return pl.pallas_call(
         reduce_kernel,
         out_shape=jax.ShapeDtypeStruct((1, LANES), F32),

time: 176 us -> 89.5 us (0.51)
  waiting for transfers between devices: 103 us -> 11.4 us
  Pallas kernels: 57.5 us -> 59.6 us
  local copies, waits for them, and re-layouts: 4.62 us -> 6.44 us
    ppermute x2 -> x5, waiting for transfers between devices: 103 us -> 11.4 us  [the longest x3 11.4 us: shifted(): lax.ppermute(value, 'chan', [(place, (place + steps) % count) for place i...]
    slice x0 -> x1, local copies, waits for them, and re-layouts: none -> 3.89 us  [on_device(): before = shifted(spectra[:, half:], 2)]
    pallas_call x3 -> x2, Pallas kernels: 37.3 us -> 41.1 us  [the longest x1 28.6 us: on_device(): pl.pallas_call(pairs_kernel, out_shape=jax.ShapeDtypeStruct((NEAR, FAR, 2...]
    ppermute x2 -> x5, starting transfers between devices: 10.5 us -> 10.5 us  [the longest x3 8.16 us: shifted(): lax.ppermute(value, 'chan', [(place, (place + steps) % count) for place i...]
  transfers between devices with their start and end apart: 2 -> 5, of which waited for: 2 -> 1; matrix products, arithmetic and copies ran while one was open for 1% -> 5% of each run, Pallas kernels for 14% -> 14%
where the time goes in v2:
time: 89.5 us; the launch traced here: 89.3 us
  Pallas kernels  59.6 us (67%)
  waiting for transfers between devices  11.4 us (13%)
  starting transfers between devices  10.5 us (12%)
  local copies, waits for them, and re-layouts  6.44 us (7%)
  other arithmetic  1.36 us (2%)
    pallas_call x1, Pallas kernels, on_device(): pl.pallas_call(pairs_kernel, out_shape=jax.ShapeDtypeStruct((NEAR, FAR, 2...  28.6 us
    pallas_call x1, Pallas kernels, on_device(): pl.pallas_call(reduce_kernel, out_shape=jax.ShapeDtypeStruct((1, LANES),...  18.6 us
    pallas_call x1, Pallas kernels, on_device(): pl.pallas_call(self_kernel, out_shape=[jax.ShapeDtypeStruct((2, half, 2 *...  12.5 us
    ppermute x3, waiting for transfers between devices, shifted(): lax.ppermute(value, 'chan', [(place, (place + steps) % count) for place i...  11.4 us
    ppermute x3, starting transfers between devices, shifted(): lax.ppermute(value, 'chan', [(place, (place + steps) % count) for place i...  8.16 us
    slice x1, local copies, waits for them, and re-layouts, on_device(): before = shifted(spectra[:, half:], 2)  3.89 us
    ppermute x2, starting transfers between devices, swapped(): lax.ppermute(value, 'chan', [(place, place ^ 1) for place in range(count)])  2.3 us
    unnamed x7, local copies, waits for them, and re-layouts  1.83 us
  transfers between devices with their start and end apart: 5, of which 1 were waited for; matrix products, arithmetic and copies ran while one was open for 5% of the time, Pallas kernels for 14%

profile of v2, /device:TPU:1, one launch (start us, length us, event | category | flops | bytes accessed | tf_op | source)
XLA Modules:
  0.0 89.3 jit_solution(341224632663710933)
XLA Ops:
  0.0 1.2 %convert.3 = bf16[1,3,256,256]{3,2,1,0:T(8,128)(2,1)S(1)} convert(s32[1,3,256,256]{3,2,1,0:T(8,128)} %param.3) | non-fusion elementwise | flops 196608 | bytes 1179648 | tf_op jit(solution)/shard_map/convert
  1.2 0.7 slice_bitcast_fusion.2
  1.9 2.0 %collective-permute-start.3 = (bf16[256,256]{1,0:T(8,128)(2,1)}, bf16[256,256]{1,0:T(8,128)(2,1)S(1)}, u32[]{:S(2)}, u32[]{:S(2)}) collective-permute-start(bf16[256,256]{1,0:T(8,128)(2,1)} %slice_bitcast_fusion.2), channel_id=1, source_target_pairs={{0,4},{4,0},{8,12},{12,8},{16,20},{20,16},{24,28},{28,24},{32,36},... | collective-permute-start | bytes 393224 | tf_op jit(solution)/shard_map/ppermute | solution.py:298
  3.9 1.7 %collective-permute-start.4 = (bf16[2,256,256]{2,1,0:T(8,128)(2,1)S(1)}, bf16[2,256,256]{2,1,0:T(8,128)(2,1)S(1)}, u32[]{:S(2)}, u32[]{:S(2)}) collective-permute-start(bf16[2,256,256]{2,1,0:T(8,128)(2,1)S(1)} %slice_bitcast_fusion), channel_id=1, source_target_pairs={{0,8},{4,12},{8,16},{12,20},{16,24},{20,28},{24,32},{28,36},{32,40... | collective-permute-start | bytes 786440 | tf_op jit(solution)/shard_map/ppermute | solution.py:293
  5.7 0.0 copy-start.1
  5.7 0.0 copy-start
  5.7 3.9 %fusion.4 = (bf16[256,16,128]{2,1,0:T(8,128)(2,1)}, bf16[256,16,128]{2,1,0:T(8,128)(2,1)}, bf16[256,16,128]{2,1,0:T(8,128)(2,1)}) fusion(bf16[256,32,128]{2,1,0:T(8,128)(2,1)} %raw.1, s32[]{:T(128)S(6)} %select_n.23), kind=kLoop, calls=%fused_computation.17 | loop fusion | bytes 6291460 | tf_op jit(solution)/shard_map/slice | solution.py:313
  9.6 1.6 %collective-permute-start.2 = (bf16[256,16,128]{2,1,0:T(8,128)(2,1)}, bf16[256,16,128]{2,1,0:T(8,128)(2,1)}, u32[]{:S(2)}, u32[]{:S(2)}) collective-permute-start(bf16[256,16,128]{2,1,0:T(8,128)(2,1)} %get-tuple-element.11), channel_id=1, source_target_pairs={{0,8},{4,12},{8,16},{12,20},{16,24},{20,28},{24,32},{28,36},{32,40... | collective-permute-start | bytes 3145736 | tf_op jit(solution)/shard_map/ppermute | solution.py:293
  11.2 0.3 collective-permute-start
  11.4 4.8 %collective-permute-start.1 = (bf16[256,16,128]{2,1,0:T(8,128)(2,1)}, bf16[256,16,128]{2,1,0:T(8,128)(2,1)}, u32[]{:S(2)}, u32[]{:S(2)}) collective-permute-start(bf16[256,16,128]{2,1,0:T(8,128)(2,1)} %get-tuple-element.13), channel_id=1, source_target_pairs={{0,248},{4,252},{8,0},{12,4},{16,8},{20,12},{24,16},{28,20},{32,24... | collective-permute-start | bytes 3145736 | tf_op jit(solution)/shard_map/ppermute | solution.py:293
  16.3 0.0 copy-done.1
  16.3 0.0 copy-done
  16.3 12.5 %shard_map.28 = (bf16[2,16,512,128]{3,2,1,0:T(8,128)(2,1)}, f32[4,2,32,64]{3,2,1,0:T(8,128)S(1)}, f32[4,64,256]{2,1,0:T(8,128)S(1)}) custom-call(bf16[256,32,128]{2,1,0:T(8,128)(2,1)S(1)} %copy-done, s32[256,256]{1,0:T(8,128)S(1)} %slice_bitcast_fusion.1.labels), custom_call_target="tpu_custom_call" | custom-call | flops 3000000000 | bytes 10000000 | tf_op jit(solution)/shard_map/pallas_call | solution.py:324
  28.8 0.2 fusion.3
  28.9 0.0 collective-permute-done.3.labels_beside
  29.0 0.0 collective-permute-done.4.labels_before
  29.0 11.4 %collective-permute-done.2.before = bf16[256,16,128]{2,1,0:T(8,128)(2,1)} collective-permute-done((bf16[256,16,128]{2,1,0:T(8,128)(2,1)}, bf16[256,16,128]{2,1,0:T(8,128)(2,1)}, u32[]{:S(2)}, u32[]{:S(2)}) %collective-permute-start.2) | collective-permute-done | bytes 1048608 | tf_op jit(solution)/shard_map/ppermute | solution.py:293
  40.3 0.0 collective-permute-done.beside
  40.3 0.0 collective-permute-done.1.after
  40.3 28.6 %shard_map.29.parts = f32[8,32,256]{2,1,0:T(8,128)S(1)} custom-call(bf16[2,16,512,128]{3,2,1,0:T(8,128)(2,1)} %get-tuple-element.8.own, bf16[256,16,128]{2,1,0:T(8,128)(2,1)} %collective-permute-done.beside, bf16[256,16,128]{2,1,0:T(8,128)(2,1)} %collective-permute-done.1.after, bf16[256,16,128]{2,1,0:T(8,128)(2,1)} %collective-permute-done.2.before, ...), custom_call_target="tpu_custom_call" | custom-call | flops 3000000000 | bytes 10000000 | tf_op jit(solution)/shard_map/pallas_call | solution.py:337
  68.9 0.0 copy-start.2
  68.9 0.7 copy-done.2
  69.6 18.6 %shard_map.30 = f32[1,128]{1,0:T(1,128)} custom-call(f32[8,32,256]{2,1,0:T(8,128)} %copy-done.2), custom_call_target="tpu_custom_call" | custom-call | tf_op jit(solution)/shard_map/pallas_call | solution.py:354
  88.2 1.1 %copy.4 = f32[1,128]{1,0:T(1,128)} copy(f32[1,128]{1,0:T(1,128)} %shard_map.30) | data formatting | bytes 1024
  (5 shorter events, 0.1 us)
Async XLA Ops:
  1.9 27.1 %collective-permute-start.3 = (bf16[256,256]{1,0:T(8,128)(2,1)}, bf16[256,256]{1,0:T(8,128)(2,1)S(1)}, u32[]{:S(2)}, u32[]{:S(2)}) collective-permute-start(bf16[256,256]{1,0:T(8,128)(2,1)} %slice_bitcast_fusion.2), channel_id=1, source_target_pairs={{0,4},{4,0},{8,12},{12,8},{16,20},{20,16},{24,28},{28,24},{32,36},... | collective-permute-start | bytes 393224 | tf_op jit(solution)/shard_map/ppermute | solution.py:298
  3.9 25.0 %collective-permute-start.4 = (bf16[2,256,256]{2,1,0:T(8,128)(2,1)S(1)}, bf16[2,256,256]{2,1,0:T(8,128)(2,1)S(1)}, u32[]{:S(2)}, u32[]{:S(2)}) collective-permute-start(bf16[2,256,256]{2,1,0:T(8,128)(2,1)S(1)} %slice_bitcast_fusion), channel_id=1, source_target_pairs={{0,8},{4,12},{8,16},{12,20},{16,24},{20,28},{24,32},{28,36},{32,40... | collective-permute-start | bytes 786440 | tf_op jit(solution)/shard_map/ppermute | solution.py:293
  5.7 10.6 %copy-start.1 = (s32[1,3,256,256]{3,2,1,0:T(8,128)S(1)}, s32[1,3,256,256]{3,2,1,0:T(8,128)}, u32[]{:S(2)}) copy-start(s32[1,3,256,256]{3,2,1,0:T(8,128)} %param.3) | copy-start | bytes 2359300
  5.7 10.6 %copy-start = (bf16[256,32,128]{2,1,0:T(8,128)(2,1)S(1)}, bf16[256,32,128]{2,1,0:T(8,128)(2,1)}, u32[]{:S(2)}) copy-start(bf16[256,32,128]{2,1,0:T(8,128)(2,1)} %raw.1) | copy-start | bytes 6291460
  9.6 30.8 %collective-permute-start.2 = (bf16[256,16,128]{2,1,0:T(8,128)(2,1)}, bf16[256,16,128]{2,1,0:T(8,128)(2,1)}, u32[]{:S(2)}, u32[]{:S(2)}) collective-permute-start(bf16[256,16,128]{2,1,0:T(8,128)(2,1)} %get-tuple-element.11), channel_id=1, source_target_pairs={{0,8},{4,12},{8,16},{12,20},{16,24},{20,28},{24,32},{28,36},{32,40... | collective-permute-start | bytes 3145736 | tf_op jit(solution)/shard_map/ppermute | solution.py:293
  11.2 29.1 %collective-permute-start = (bf16[256,16,128]{2,1,0:T(8,128)(2,1)}, bf16[256,16,128]{2,1,0:T(8,128)(2,1)}, u32[]{:S(2)}, u32[]{:S(2)}) collective-permute-start(bf16[256,16,128]{2,1,0:T(8,128)(2,1)} %get-tuple-element.12), channel_id=1, source_target_pairs={{0,4},{4,0},{8,12},{12,8},{16,20},{20,16},{24,28},{28,24},{32,36},... | collective-permute-start | bytes 3145736 | tf_op jit(solution)/shard_map/ppermute | solution.py:298
  11.4 28.9 %collective-permute-start.1 = (bf16[256,16,128]{2,1,0:T(8,128)(2,1)}, bf16[256,16,128]{2,1,0:T(8,128)(2,1)}, u32[]{:S(2)}, u32[]{:S(2)}) collective-permute-start(bf16[256,16,128]{2,1,0:T(8,128)(2,1)} %get-tuple-element.13), channel_id=1, source_target_pairs={{0,248},{4,252},{8,0},{12,4},{16,8},{20,12},{24,16},{28,20},{32,24... | collective-permute-start | bytes 3145736 | tf_op jit(solution)/shard_map/ppermute | solution.py:293
  68.9 0.7 copy-start.2

commit v3 on v2

v3 whole, which is shorter than its diff:
```python
import functools
import math

import jax
import jax.numpy as jnp
import numpy as np
from jax import lax
from jax.experimental import pallas as pl
from jax.experimental.pallas import tpu as pltpu
from jax.sharding import PartitionSpec as P

F32 = jnp.float32
BF16 = jnp.bfloat16
MESH = pl.DeviceIdType.MESH
VMEM = pl.BlockSpec(memory_space=pltpu.VMEM)
ANY = pl.BlockSpec(memory_space=pl.ANY)
DMA = pltpu.SemaphoreType.DMA

CH = 256
LANES = 128
HALF = LANES // 2
SEGMENTS = 4
CLASSES = 64
PAD = 8
NEAR = 8
FAR = 32
FREQ_UNROLL = 8
ROW_UNROLL = 64
SELF_UNROLL = 32
COUNT_ROWS = 8


def whiten(raw, rows, white, with_rotated):
    freqs = raw.shape[1]
    step = freqs + PAD
    chunk = 32

    def normalise(block, _):
        values = raw[pl.ds(block * chunk, chunk)].astype(F32)
        meansq = jnp.mean(values * values, axis=-1, keepdims=True)
        scaled = values * lax.rsqrt(meansq + 1e-05)
        for channel in range(chunk):
            start = pl.multiple_of((block * chunk + channel) * step, 8)
            rows[pl.ds(start, freqs), :] = scaled[channel]
        return 0

    lax.fori_loop(0, CH // chunk, normalise, 0)

    def regroup(block, _):
        for part in range(FREQ_UNROLL):
            freq = block * FREQ_UNROLL + part
            values = rows[pl.ds(freq, CH, stride=step), :]
            white[freq, :CH, :] = values.astype(BF16)
            if with_rotated:
                lane = lax.broadcasted_iota(jnp.int32, (CH, LANES), 1)
                turned = pltpu.roll(values, HALF, 1)
                white[freq, CH:, :] = jnp.where(lane < HALF, turned, -turned).astype(BF16)
        return 0

    lax.fori_loop(0, freqs // FREQ_UNROLL, regroup, 0)


def cross_pairs(first, second, cross, top):
    freqs = second.shape[0]
    step = CH + PAD

    def body(block, _):
        for part in range(FREQ_UNROLL):
            freq = block * FREQ_UNROLL + part
            product = lax.dot_general(
                first[freq], second[freq, :CH, :], (((1,), (1,)), ((), ())), preferred_element_type=F32
            )
            for row in range(2):
                start = pl.multiple_of((top + freq + row * freqs) * step, 8)
                for side in range(2):
                    cross[side, pl.ds(start, CH), :] = product[
                        row * CH : (row + 1) * CH, side * LANES : (side + 1) * LANES
                    ]
        return 0

    lax.fori_loop(0, freqs // FREQ_UNROLL, body, 0)


def add_bins(cross, read_labels, weight, slots, nrows, add_sums, counts):
    step = CH + PAD
    slot_ids = slot_numbers()
    one = jnp.ones((), BF16)
    zero = jnp.zeros((), BF16)
    segments = read_labels() & (SEGMENTS - 1)
    first, last = jnp.min(segments), jnp.max(segments)

    def add_segment(segment, _):
        marks = read_labels()
        slots[...] = jnp.where((marks & (SEGMENTS - 1)) == segment, slots_of(marks), -1.0)

        def add_rows(block, _):
            pieces, onehots = [], []
            tally = None
            for part in range(ROW_UNROLL):
                i = block * ROW_UNROLL + part
                sides = [cross[side, pl.ds(i, nrows, stride=step), :] for side in range(2)]
                pieces.append(jnp.concatenate(sides, axis=1).astype(BF16))
                row = jnp.broadcast_to(slots[pl.ds(i, 1), :], (16, CH)).astype(BF16)
                onehot = jnp.where(row[None] == slot_ids, one, zero).reshape(CLASSES, CH)
                onehots.append(onehot)
                tally = onehot if tally is None else tally + onehot
            add_sums(
                segment,
                lax.dot_general(
                    jnp.concatenate(pieces, axis=1),
                    jnp.concatenate(onehots, axis=1),
                    (((1,), (1,)), ((), ())),
                    preferred_element_type=F32,
                ),
            )
            counts[segment] += tally.astype(F32) * weight
            return 0

        lax.fori_loop(0, CH // ROW_UNROLL, add_rows, 0)
        return 0

    lax.fori_loop(first, last + 1, add_segment, 0)


def slot_numbers():
    shape = (CLASSES // 16, 16, CH)
    ids = lax.broadcasted_iota(jnp.int32, shape, 0) * 16 + lax.broadcasted_iota(jnp.int32, shape, 1)
    return ids.astype(F32).astype(BF16)


def slots_of(marks):
    classes = lax.shift_right_logical(marks, 2)
    return ((classes & 1) * (CLASSES // 2) + lax.shift_right_logical(classes, 1)).astype(F32)


def add_all_bins(cross, slots, segments, nrows, sums, tally):
    step = CH + PAD
    slot_ids = slot_numbers()
    row_ids = lax.broadcasted_iota(jnp.int32, (16, CH), 0).astype(F32).astype(BF16)
    one = jnp.ones((), BF16)
    zero = jnp.zeros((), BF16)

    def add_rows(block, _):
        pieces, onehots = [], []
        for part in range(SELF_UNROLL):
            i = block * SELF_UNROLL + part
            sides = [cross[side, pl.ds(i, nrows, stride=step), :] for side in range(2)]
            values = jnp.concatenate(sides, axis=1).astype(BF16).reshape(nrows // 16, 16, CH)
            place = jnp.broadcast_to(segments[pl.ds(i, 1), :], (16, CH)).astype(BF16)
            masked = [
                jnp.where(place[None] == jnp.full((), segment, BF16), values, zero).reshape(nrows, CH)
                for segment in range(SEGMENTS)
            ]
            masked.append(jnp.where(place == row_ids, one, zero))
            pieces.append(jnp.concatenate(masked, axis=0))
            row = jnp.broadcast_to(slots[pl.ds(i, 1), :], (16, CH)).astype(BF16)
            onehots.append(jnp.where(row[None] == slot_ids, one, zero).reshape(CLASSES, CH))
        binned = lax.dot_general(
            jnp.concatenate(pieces, axis=1),
            jnp.concatenate(onehots, axis=1),
            (((1,), (1,)), ((), ())),
            preferred_element_type=F32,
        )
        for segment in range(SEGMENTS):
            sums[segment] += binned[segment * nrows : (segment + 1) * nrows].reshape(sums.shape[1:])
        tally[...] += binned[SEGMENTS * nrows :]
        return 0

    lax.fori_loop(0, CH // SELF_UNROLL, add_rows, 0)


def exchange_kernel(
    spectra, pair_bins, after, before, beside, labels_before, labels_beside, white_out, sums, tally,
    raw, labels, sent_labels, white, rows, cross, slots, segments, local_sem, send_sem, recv_sem,
):
    half = white.shape[1]
    chan, off = lax.axis_index("chan"), lax.axis_index("off")
    count = lax.axis_size("chan")
    low = lax.rem(chan, 2)
    down, up = lax.rem(chan + count - 2, count), lax.rem(chan + 2, count)
    partner = chan + 1 - 2 * low
    load_raw = pltpu.make_async_copy(spectra, raw, local_sem.at[0])
    load_labels = pltpu.make_async_copy(pair_bins.at[0], labels, local_sem.at[1])
    load_labels.start()
    load_raw.start()
    barrier = pltpu.get_barrier_semaphore()
    for neighbour in (partner, down, up):
        pl.semaphore_signal(barrier, inc=1, device_id=(neighbour, off), device_id_type=MESH)
    pl.semaphore_wait(barrier, 3)

    def send(index, source, target, chan_to):
        copy = pltpu.make_async_remote_copy(
            src_ref=source,
            dst_ref=target,
            send_sem=send_sem.at[index],
            recv_sem=recv_sem.at[index],
            device_id=(chan_to, off),
            device_id_type=MESH,
        )
        copy.start()
        return copy

    other_half = pl.ds(pl.multiple_of((1 - low) * half, half), half)
    copies = [
        send(0, spectra.at[:, half : 2 * half, :], before, up),
        send(1, spectra.at[:, 0:half, :], after, down),
        send(2, spectra.at[:, other_half, :], beside, partner),
    ]
    load_labels.wait()
    sent_labels[...] = labels[1:].astype(F32).astype(BF16)
    copies.append(send(3, sent_labels, labels_before, up))
    copies.append(send(4, sent_labels.at[0], labels_beside, partner))
    marks = labels[0]
    slots[...] = slots_of(marks)
    segments[...] = (marks & (SEGMENTS - 1)).astype(F32)
    sums[...] = jnp.zeros_like(sums)
    tally[...] = jnp.zeros_like(tally)
    load_raw.wait()
    whiten(raw, rows, white.reshape(2 * half, 2 * CH, LANES), True)
    keep = pltpu.make_async_copy(white, white_out, local_sem.at[2])
    keep.start()
    for side in range(2):
        cross_pairs(white.at[side], white.at[side], cross, side * 2 * half)
    add_all_bins(cross, slots, segments, 4 * half, sums, tally)
    keep.wait()
    for copy in copies:
        copy.wait()


def pairs_kernel(
    own, beside, after, before, labels, labels_beside, labels_before, sums_in,
    sums, counts, white, raw, rows, cross, slots, load_sem,
):
    half = own.shape[1]
    loads = [
        pltpu.make_async_copy(block, raw.at[index], load_sem.at[index])
        for index, block in enumerate((beside, after, before))
    ]
    load_own = pltpu.make_async_copy(own, white.at[0:2], load_sem.at[3])
    for load in loads:
        load.start()
    load_own.start()
    sums[...] = sums_in[...]
    counts[...] = jnp.zeros_like(counts)
    for index, load in enumerate(loads):
        load.wait()
        whiten(raw.at[index], rows, white.at[2 + index], index != 1)
    load_own.wait()
    low = lax.rem(lax.axis_index("chan"), 2)
    counted = (lax.axis_index("off") == 0).astype(F32)
    even = (1 - low).astype(F32) * counted
    odd = low.astype(F32) * counted

    def moved(ref):
        return ref[...].astype(F32).astype(jnp.int32)

    def choose(if_even, if_odd):
        return lambda: jnp.where(low == 0, if_even(), if_odd())

    own_near, own_far = lambda: labels[1], lambda: labels[2]
    beside_near = lambda: moved(labels_beside)
    before_near, before_far = lambda: moved(labels_before.at[0]), lambda: moved(labels_before.at[1])
    jobs = (
        ((0, 2), (2, 1), choose(own_near, beside_near), low, even),
        ((0, 3), (4, 1), choose(own_far, before_far), low, even),
        ((2, 3), (4, 2), choose(beside_near, before_near), low, even),
        ((4, 1), (0, 3), choose(before_far, own_far), 1 - low, odd),
    )
    for if_even, if_odd, read_labels, side, weight in jobs:
        first = if_even[0] + low * (if_odd[0] - if_even[0])
        second = if_even[1] + low * (if_odd[1] - if_even[1])
        cross_pairs(white.at[first], white.at[second], cross, 0)

        def add_sums(segment, values):
            sums[segment, side] += values

        add_bins(cross, read_labels, weight, slots, 2 * half, add_sums, counts)


def reduce_kernel(
    sums, counts, self_tally, table, out, parts, near_in, far_out, far_in, near_send, near_recv, far_send, far_recv
):
    chan, off = lax.axis_index("chan"), lax.axis_index("off")
    low, high = lax.rem(chan, 2), lax.div(chan, 2)
    near = off * 2 + low

    def near_device(step):
        index = lax.rem(near + step, NEAR)
        return index, (high * 2 + lax.rem(index, 2), lax.div(index, 2))

    def far_device(step):
        index = lax.rem(high + step, FAR)
        return index, (index * 2 + low, off)

    barrier = pltpu.get_barrier_semaphore()

    def greet_near(step, _):
        pl.semaphore_signal(barrier, inc=1, device_id=near_device(step)[1], device_id_type=MESH)
        return 0

    def greet_far(step, _):
        pl.semaphore_signal(barrier, inc=1, device_id=far_device(step)[1], device_id_type=MESH)
        return 0

    lax.fori_loop(1, NEAR, greet_near, 0)
    lax.fori_loop(1, FAR, greet_far, 0)
    ones = jnp.ones((COUNT_ROWS, CH), F32)
    for segment in range(SEGMENTS):
        trace = lax.dot_general(
            sums[segment].reshape(table.shape[1], CLASSES),
            table[off],
            (((0,), (0,)), ((), ())),
            precision=lax.Precision.HIGHEST,
            preferred_element_type=F32,
        )
        tally = lax.dot_general(
            ones,
            counts[segment],
            (((1,), (1,)), ((), ())),
            precision=lax.Precision.HIGHEST,
            preferred_element_type=F32,
        )
        own = self_tally[segment : segment + 1, :] * (off == 0).astype(F32)
        tally = tally + jnp.broadcast_to(own, tally.shape)
        tally = jnp.concatenate([tally, jnp.zeros((COUNT_ROWS, LANES - CLASSES), F32)], axis=1)
        for part in range(2):
            parts[segment * 2 + part, :FAR, :] = trace[part * FAR : (part + 1) * FAR]
            parts[segment * 2 + part, FAR:, :] = tally
    pl.semaphore_wait(barrier, FAR - 1 + NEAR - 1)

    def near_copy(step):
        index, device = near_device(step)
        return pltpu.make_async_remote_copy(
            src_ref=parts.at[index],
            dst_ref=near_in.at[step - 1],
            send_sem=near_send.at[step - 1],
            recv_sem=near_recv.at[step - 1],
            device_id=device,
            device_id_type=MESH,
        )

    def far_copy(step):
        index, device = far_device(step)
        return pltpu.make_async_remote_copy(
            src_ref=far_out.at[index],
            dst_ref=far_in.at[step - 1],
            send_sem=far_send.at[step - 1],
            recv_sem=far_recv.at[step - 1],
            device_id=device,
            device_id_type=MESH,
        )

    def start_near(step, _):
        near_copy(step).start()
        return 0

    def start_far(step, _):
        far_copy(step).start()
        return 0

    lax.fori_loop(1, NEAR, start_near, 0)

    def add_near(step, total):
        near_copy(step).wait_recv()
        return total + near_in[step - 1]

    total = lax.fori_loop(1, NEAR, add_near, parts[near])
    for row in range(FAR):
        far_out[row] = jnp.concatenate([total[row : row + 1], total[FAR : FAR + 1]], axis=1)
    lax.fori_loop(1, FAR, start_far, 0)

    def add_far(step, total):
        far_copy(step).wait_recv()
        return total + far_in[step - 1]

    total = lax.fori_loop(1, FAR, add_far, far_out[high])
    lane = lax.broadcasted_iota(jnp.int32, (1, LANES), 1)
    count = jnp.sum(jnp.where(lane == low * FAR + high, total[:, LANES:], 0.0), axis=1, keepdims=True)
    out[...] = total[:, :LANES] / jnp.sqrt(jnp.maximum(count, 1.0))

    def end_near(step, _):
        near_copy(step).wait_send()
        return 0

    def end_far(step, _):
        far_copy(step).wait_send()
        return 0

    lax.fori_loop(1, NEAR, end_near, 0)
    lax.fori_loop(1, FAR, end_far, 0)


def lag_tables(groups, freqs, lags):
    nfreq = groups * freqs
    shifts = np.arange(lags) - lags // 2
    theta = math.pi * np.mod(np.arange(nfreq)[:, None] * shifts[None, :], 2 * nfreq) / nfreq
    table = np.stack([np.cos(theta), -np.sin(theta)]).reshape(2, groups, 2, freqs // 2, lags)
    table = table.transpose(1, 2, 0, 3, 4).reshape(groups, 2 * freqs, lags)
    return jnp.asarray((table / HALF).astype(np.float32))


def on_device(spectra, pair_bins):
    freqs = spectra.shape[1]
    half = freqs // 2
    vmem_limit = 56 * 1024 * 1024
    white_shape = jax.ShapeDtypeStruct((2, half, 2 * CH, LANES), BF16)
    block_shape = jax.ShapeDtypeStruct((CH, half, LANES), BF16)
    sums_shape = jax.ShapeDtypeStruct((SEGMENTS, 2, 2 * half, CLASSES), F32)
    counts_shape = jax.ShapeDtypeStruct((SEGMENTS, CLASSES, CH), F32)
    square = pltpu.VMEM((CH, CH), F32)

    after, before, beside, labels_before, labels_beside, white, sums, tally = pl.pallas_call(
        exchange_kernel,
        out_shape=[
            block_shape,
            block_shape,
            block_shape,
            jax.ShapeDtypeStruct((2, CH, CH), BF16),
            jax.ShapeDtypeStruct((CH, CH), BF16),
            white_shape,
            sums_shape,
            jax.ShapeDtypeStruct((16, CLASSES), F32),
        ],
        in_specs=[ANY] * 2,
        out_specs=[ANY] * 6 + [VMEM] * 2,
        scratch_shapes=[
            pltpu.VMEM(spectra.shape, BF16),
            pltpu.VMEM(pair_bins.shape[1:], jnp.int32),
            pltpu.VMEM((2, CH, CH), BF16),
            pltpu.VMEM(white_shape.shape, BF16),
            pltpu.VMEM((CH * (freqs + PAD), LANES), F32),
            pltpu.VMEM((2, 2 * freqs * (CH + PAD), LANES), F32),
            square,
            square,
            DMA((3,)),
            DMA((5,)),
            DMA((5,)),
        ],
        compiler_params=pltpu.CompilerParams(
            collective_id=1, has_side_effects=True, vmem_limit_bytes=vmem_limit
        ),
    )(spectra, pair_bins)
    sums, counts = pl.pallas_call(
        pairs_kernel,
        out_shape=[sums_shape, counts_shape],
        in_specs=[ANY] * 4 + [VMEM] * 4,
        out_specs=[VMEM] * 2,
        scratch_shapes=[
            pltpu.VMEM((5, half, 2 * CH, LANES), BF16),
            pltpu.VMEM((3, CH, half, LANES), BF16),
            pltpu.VMEM((CH * (half + PAD), LANES), F32),
            pltpu.VMEM((2, 2 * half * (CH + PAD), LANES), F32),
            square,
            DMA((4,)),
        ],
        compiler_params=pltpu.CompilerParams(vmem_limit_bytes=vmem_limit),
    )(white, beside, after, before, pair_bins[0], labels_beside, labels_before, sums)
    return pl.pallas_call(
        reduce_kernel,
        out_shape=jax.ShapeDtypeStruct((1, LANES), F32),
        in_specs=[VMEM] * 4,
        out_specs=VMEM,
        scratch_shapes=[
            pltpu.VMEM((NEAR, FAR + COUNT_ROWS, LANES), F32),
            pltpu.VMEM((NEAR - 1, FAR + COUNT_ROWS, LANES), F32),
            pltpu.VMEM((FAR, 1, 2 * LANES), F32),
            pltpu.VMEM((FAR - 1, 1, 2 * LANES), F32),
            DMA((NEAR - 1,)),
            DMA((NEAR - 1,)),
            DMA((FAR - 1,)),
            DMA((FAR - 1,)),
        ],
        compiler_params=pltpu.CompilerParams(collective_id=0, has_side_effects=True),
    )(sums, counts, tally, lag_tables(lax.axis_size("off"), freqs, LANES))


def solution(mesh):
    in_specs = (P("chan", "off", None), P("chan", None, None, None))
    out_specs = P(("chan", "off"), None)
    return jax.shard_map(
        on_device, mesh=mesh, in_specs=in_specs, out_specs=out_specs, check_vma=False
    )
```

time: 89.5 us -> 86.8 us (0.970)
  Pallas kernels: 59.6 us -> 85.4 us
  waiting for transfers between devices: 11.4 us -> 0 us
  starting transfers between devices: 10.5 us -> 0 us
  local copies, waits for them, and re-layouts: 6.44 us -> 1.14 us
  other arithmetic: 1.36 us -> 0 us
    pallas_call x2, Pallas kernels: 41.1 us -> 67.1 us  [the longest x1 39.3 us: on_device(): pl.pallas_call(exchange_kernel, out_shape=[block_shape, block_shape, bloc...]
    ppermute x5 -> x0, waiting for transfers between devices: 11.4 us -> none  [the longest x3 11.4 us: shifted(): lax.ppermute(value, 'chan', [(place, (place + steps) % count) for place i...]
    ppermute x5 -> x0, starting transfers between devices: 10.5 us -> none  [the longest x3 8.16 us: shifted(): lax.ppermute(value, 'chan', [(place, (place + steps) % count) for place i...]
    slice x1 -> x0, local copies, waits for them, and re-layouts: 3.89 us -> none  [on_device(): before = shifted(spectra[:, half:], 2)]
    another operation x1 -> x0, other arithmetic: 1.19 us -> none
    unnamed x7 -> x1, local copies, waits for them, and re-layouts: 1.83 us -> 1.14 us
  transfers between devices with their start and end apart: 5 -> 0, of which waited for: 1 -> 0; matrix products, arithmetic and copies ran while one was open for 5% -> 0% of each run, Pallas kernels for 14% -> 0%
where the time goes in v3:
time: 86.8 us; the launch traced here: 86.6 us
  Pallas kernels  85.4 us (98%)
  local copies, waits for them, and re-layouts  1.14 us (1%)
    pallas_call x1, Pallas kernels, on_device(): pl.pallas_call(exchange_kernel, out_shape=[block_shape, block_shape, bloc...  39.3 us
    pallas_call x1, Pallas kernels, on_device(): pl.pallas_call(pairs_kernel, out_shape=[sums_shape, counts_shape], in_spe...  27.7 us
    pallas_call x1, Pallas kernels, on_device(): pl.pallas_call(reduce_kernel, out_shape=jax.ShapeDtypeStruct((1, LANES),...  18.4 us

profile of v3, /device:TPU:1, one launch (start us, length us, event | category | flops | bytes accessed | tf_op | source)
XLA Modules:
  0.0 86.6 jit_solution(15105789541450934587)
XLA Ops:
  0.0 39.3 %shard_map.37 = (bf16[256,16,128]{2,1,0:T(8,128)(2,1)}, bf16[256,16,128]{2,1,0:T(8,128)(2,1)}, bf16[256,16,128]{2,1,0:T(8,128)(2,1)}, bf16[2,256,256]{2,1,0:T(8,...) custom-call(bf16[256,32,128]{2,1,0:T(8,128)(2,1)} %spectra.1, ...), custom_call_target="tpu_custom_call" | custom-call | tf_op jit(solution)/shard_map/pallas_call | solution.py:412
  39.3 27.7 %shard_map.38 = (f32[4,2,32,64]{3,2,1,0:T(8,128)}, f32[4,64,256]{2,1,0:T(8,128)}) custom-call(bf16[2,16,512,128]{3,2,1,0:T(8,128)(2,1)} %get-tuple-element.15.own, bf16[256,16,128]{2,1,0:T(8,128)(2,1)} %get-tuple-element.16.beside, bf16[256,16,128]{2,1,0:T(8,128)(2,1)} %get-tuple-element.17.after, bf16[256,16,128]{2,1,0:T(8,128)(2,1)} %get-tuple-element.18.before, ...), custom_call_target="tpu_custom_call" | custom-call | tf_op jit(solution)/shard_map/pallas_call | solution.py:443
  67.1 18.4 %shard_map.39 = f32[1,128]{1,0:T(1,128)} custom-call(f32[4,2,32,64]{3,2,1,0:T(8,128)} %get-tuple-element.22.sums, f32[4,64,256]{2,1,0:T(8,128)} %get-tuple-element.23.counts, f32[16,64]{1,0:T(8,128)} %get-tuple-element.24.self_tally, f32[4,64,128]{2,1,0:T(8,128)} %constant.2.clone.table), custom_call_target="tpu_custom_call" | custom-call | tf_op jit(solution)/shard_map/pallas_call | solution.py:458
  85.5 1.1 %copy.5 = f32[1,128]{1,0:T(1,128)} copy(f32[1,128]{1,0:T(1,128)} %shard_map.39) | data formatting | bytes 1024

commit v4 on v3

v4 whole, which is shorter than its diff:
```python
import functools
import math

import jax
import jax.numpy as jnp
import numpy as np
from jax import lax
from jax.experimental import pallas as pl
from jax.experimental.pallas import tpu as pltpu
from jax.sharding import PartitionSpec as P

F32 = jnp.float32
BF16 = jnp.bfloat16
MESH = pl.DeviceIdType.MESH
VMEM = pl.BlockSpec(memory_space=pltpu.VMEM)
ANY = pl.BlockSpec(memory_space=pl.ANY)
DMA = pltpu.SemaphoreType.DMA

CH = 256
LANES = 128
EARLY = CH // 2
HALF = LANES // 2
SEGMENTS = 4
CLASSES = 64
PAD = 8
NEAR = 8
FAR = 32
FREQ_UNROLL = 8
ROW_UNROLL = 64
SELF_UNROLL = 32
COUNT_ROWS = 8


def whiten(raw, rows, white, with_rotated):
    channels, freqs, _ = raw.shape
    step = freqs + PAD
    chunk = 32

    def normalise(block, _):
        values = raw[pl.ds(block * chunk, chunk)].astype(F32)
        meansq = jnp.mean(values * values, axis=-1, keepdims=True)
        scaled = values * lax.rsqrt(meansq + 1e-05)
        for channel in range(chunk):
            start = pl.multiple_of((block * chunk + channel) * step, 8)
            rows[pl.ds(start, freqs), :] = scaled[channel]
        return 0

    lax.fori_loop(0, channels // chunk, normalise, 0)

    def regroup(block, _):
        for part in range(FREQ_UNROLL):
            freq = block * FREQ_UNROLL + part
            values = rows[pl.ds(freq, channels, stride=step), :]
            white[freq, 0] = values.astype(BF16)
            if with_rotated:
                lane = lax.broadcasted_iota(jnp.int32, (channels, LANES), 1)
                turned = pltpu.roll(values, HALF, 1)
                white[freq, 1] = jnp.where(lane < HALF, turned, -turned).astype(BF16)
        return 0

    lax.fori_loop(0, freqs // FREQ_UNROLL, regroup, 0)


def cross_pairs(first, second, cross, freqs, top=0):
    step = CH + PAD

    def body(block, _):
        for part in range(FREQ_UNROLL):
            freq = block * FREQ_UNROLL + part
            product = lax.dot_general(
                first(freq), second(freq), (((1,), (1,)), ((), ())), preferred_element_type=F32
            )
            for row in range(2):
                start = pl.multiple_of((top + freq + row * freqs) * step, 8)
                for side in range(product.shape[1] // LANES):
                    cross[side, pl.ds(start, CH), :] = product[
                        row * CH : (row + 1) * CH, side * LANES : (side + 1) * LANES
                    ]
        return 0

    lax.fori_loop(0, freqs // FREQ_UNROLL, body, 0)


def slot_numbers(width):
    shape = (CLASSES // 16, 16, width)
    ids = lax.broadcasted_iota(jnp.int32, shape, 0) * 16 + lax.broadcasted_iota(jnp.int32, shape, 1)
    return ids.astype(F32).astype(BF16)


def slots_of(marks):
    classes = lax.shift_right_logical(marks, 2)
    return ((classes & 1) * (CLASSES // 2) + lax.shift_right_logical(classes, 1)).astype(F32)


def piece_of(cross, i, nrows, width):
    sides = [cross[side, pl.ds(i, nrows, stride=CH + PAD), :] for side in range(width // LANES)]
    return jnp.concatenate(sides, axis=1).astype(BF16)


def row_of(ref, i, width):
    return jnp.broadcast_to(ref[pl.ds(i, 1), :][:, :width], (16, width)).astype(BF16)


def add_bins(cross, read_labels, width, weight, slots, nrows, add_sums, counts):
    slot_ids = slot_numbers(width)
    unroll = ROW_UNROLL * CH // width
    one = jnp.ones((), BF16)
    zero = jnp.zeros((), BF16)
    segments = read_labels() & (SEGMENTS - 1)
    first, last = jnp.min(segments), jnp.max(segments)

    def add_segment(segment, _):
        marks = read_labels()
        slots[:, :width] = jnp.where((marks & (SEGMENTS - 1)) == segment, slots_of(marks), -1.0)

        def add_rows(block, _):
            pieces, onehots = [], []
            tally = None
            for part in range(unroll):
                i = block * unroll + part
                pieces.append(piece_of(cross, i, nrows, width))
                row = row_of(slots, i, width)
                onehot = jnp.where(row[None] == slot_ids, one, zero).reshape(CLASSES, width)
                onehots.append(onehot)
                tally = onehot if tally is None else tally + onehot
            add_sums(
                segment,
                lax.dot_general(
                    jnp.concatenate(pieces, axis=1),
                    jnp.concatenate(onehots, axis=1),
                    (((1,), (1,)), ((), ())),
                    preferred_element_type=F32,
                ),
            )
            counts[segment, :, :width] += tally.astype(F32) * weight
            return 0

        lax.fori_loop(0, CH // unroll, add_rows, 0)
        return 0

    lax.fori_loop(first, last + 1, add_segment, 0)


def add_all_bins(cross, slots, segments, width, nrows, add_sums, add_tally, begin=0, end=CH):
    slot_ids = slot_numbers(width)
    unroll = SELF_UNROLL * CH // width
    row_ids = lax.broadcasted_iota(jnp.int32, (16, width), 0).astype(F32).astype(BF16)
    one = jnp.ones((), BF16)
    zero = jnp.zeros((), BF16)

    def add_rows(block, _):
        pieces, onehots = [], []
        for part in range(unroll):
            i = block * unroll + part
            values = piece_of(cross, i, nrows, width).reshape(nrows // 16, 16, width)
            place = row_of(segments, i, width)
            masked = [
                jnp.where(place[None] == jnp.full((), segment, BF16), values, zero).reshape(nrows, width)
                for segment in range(SEGMENTS)
            ]
            masked.append(jnp.where(place == row_ids, one, zero))
            pieces.append(jnp.concatenate(masked, axis=0))
            row = row_of(slots, i, width)
            onehots.append(jnp.where(row[None] == slot_ids, one, zero).reshape(CLASSES, width))
        binned = lax.dot_general(
            jnp.concatenate(pieces, axis=1),
            jnp.concatenate(onehots, axis=1),
            (((1,), (1,)), ((), ())),
            preferred_element_type=F32,
        )
        for segment in range(SEGMENTS):
            add_sums(segment, binned[segment * nrows : (segment + 1) * nrows])
        add_tally(binned[SEGMENTS * nrows :])
        return 0

    lax.fori_loop(begin // unroll, end // unroll, add_rows, 0)


def as_integers(values):
    return values.astype(F32).astype(jnp.int32)


def turned_back(values, side):
    half = values.shape[0] // 2
    sign = (1 - 2 * side).astype(F32)
    return jnp.concatenate([values[:half], values[half:] * sign], axis=0)


def exchange_kernel(
    spectra, pair_bins, after, before, beside, white_out, early_out, labels_before, labels_beside, sums, tally,
    raw, early_raw, labels, sent_labels, white, early, rows, cross, slots, segments,
    local_sem, send_sem, recv_sem,
):
    half = white.shape[1]
    chan, off = lax.axis_index("chan"), lax.axis_index("off")
    count = lax.axis_size("chan")
    low = lax.rem(chan, 2)
    even, odd = (1 - low).astype(F32), low.astype(F32)
    down, up = lax.rem(chan + count - 2, count), lax.rem(chan + 2, count)
    partner = chan + 1 - 2 * low
    load_raw = pltpu.make_async_copy(spectra, raw, local_sem.at[0])
    load_labels = pltpu.make_async_copy(pair_bins.at[0], labels, local_sem.at[1])
    load_labels.start()
    load_raw.start()
    barrier = pltpu.get_barrier_semaphore()
    for neighbour in (partner, down, up):
        pl.semaphore_signal(barrier, inc=1, device_id=(neighbour, off), device_id_type=MESH)
    pl.semaphore_wait(barrier, 3)

    def remote(index, source, target, chan_to):
        return pltpu.make_async_remote_copy(
            src_ref=source,
            dst_ref=target,
            send_sem=send_sem.at[index],
            recv_sem=recv_sem.at[index],
            device_id=(chan_to, off),
            device_id_type=MESH,
        )

    other_half = pl.ds(pl.multiple_of((1 - low) * half, half), half)
    copies = []
    for piece in range(2):
        part = slice(piece * EARLY, (piece + 1) * EARLY)
        copies.append(
            [
                remote(3 * piece, spectra.at[part, other_half, :], beside.at[part], partner),
                remote(3 * piece + 1, spectra.at[part, 0:half, :], after.at[part], down),
                remote(3 * piece + 2, spectra.at[part, half : 2 * half, :], before.at[part], up),
            ]
        )
    for copy in copies[0]:
        copy.start()
    load_labels.wait()
    near, far = labels[1].astype(F32), labels[2].astype(F32)
    near_turned = near.T
    sent_labels[0] = near_turned.astype(BF16)
    sent_labels[1] = far.T.astype(BF16)
    sent_labels[2] = jnp.where(low == 0, near_turned, near).astype(BF16)
    label_copies = [
        remote(6, sent_labels.at[1], labels_before.at[1], up),
        remote(7, sent_labels.at[2], labels_beside, partner),
    ]
    for copy in label_copies:
        copy.start()
    near_copy = remote(8, sent_labels.at[0], labels_before.at[0], up)

    @pl.when(low == 1)
    def _():
        near_copy.start()

    marks = labels[0]
    slots[...] = slots_of(marks)
    segments[...] = (marks & (SEGMENTS - 1)).astype(F32)
    sums[...] = jnp.zeros_like(sums)
    tally[...] = jnp.zeros_like(tally)
    load_raw.wait()
    whiten(raw, rows, white.reshape(2 * half, 2, CH, LANES), True)
    keep = pltpu.make_async_copy(white, white_out, local_sem.at[2])
    keep.start()

    def own(side):
        return lambda freq: white[side, freq].reshape(2 * CH, LANES)

    for side in range(2):
        cross_pairs(own(side), lambda freq, side=side: white[side, freq, 0], cross, half, side * 2 * half)

    def add_self(segment, values):
        sums[segment] += values.reshape(2, 2 * half, CLASSES)

    def add_tally(weight):
        def add(values):
            tally[...] += values * weight

        return add

    bin_self = functools.partial(
        add_all_bins, cross, slots, segments, CH, 4 * half, add_self, add_tally(1.0)
    )
    bin_self(begin=0, end=CH // 2)
    for copy in copies[1]:
        copy.start()
    bin_self(begin=CH // 2, end=CH)

    loads = []
    for index, (copy, block) in enumerate(zip(copies[0], (beside, after, before))):
        copy.wait_recv()
        load = pltpu.make_async_copy(block.at[0:EARLY], early_raw.at[index], local_sem.at[3 + index])
        load.start()
        loads.append(load)
    for index, load in enumerate(loads):
        load.wait()
        whiten(early_raw.at[index], rows, early.at[index], index == 0)
    keep_early = pltpu.make_async_copy(early, early_out, local_sem.at[6])
    keep_early.start()
    for copy in label_copies:
        copy.wait_recv()
    before_far, beside_near = as_integers(labels_before[1]), as_integers(labels_beside[...])
    own_near, own_far = labels[1], labels[2]
    marks = jnp.concatenate(
        [
            jnp.where(low == 0, own_near, beside_near)[:, :LANES],
            jnp.where(low == 0, own_far, before_far)[:, :LANES],
        ],
        axis=1,
    )
    slots[...] = slots_of(marks)
    segments[...] = (marks & (SEGMENTS - 1)).astype(F32)

    def add_to(side):
        def add(segment, values):
            sums[segment, side] += turned_back(values, side)

        return add

    cross_pairs(
        own(low),
        lambda freq: jnp.concatenate([early[0, freq, 0], early[1 + low, freq, 0]], axis=0),
        cross,
        half,
    )
    add_all_bins(cross, slots, segments, CH, 2 * half, add_to(low), add_tally(even))
    marks = jnp.where(low == 0, before_far, own_far)[:, :LANES]
    slots[:, :LANES] = slots_of(marks)
    segments[:, :LANES] = (marks & (SEGMENTS - 1)).astype(F32)
    cross_pairs(own(1 - low), lambda freq: early[2 - low, freq, 0], cross, half)
    add_all_bins(cross, slots, segments, LANES, 2 * half, add_to(1 - low), add_tally(odd))

    keep.wait()
    keep_early.wait()
    for copy in copies[1]:
        copy.wait_recv()
    for copy in copies[0] + copies[1] + label_copies:
        copy.wait_send()

    @pl.when(low == 1)
    def _():
        near_copy.wait()


def pairs_kernel(
    own, early, beside, after, before, labels, labels_beside, labels_before, sums_in,
    sums, counts, white, blocks, raw, rows, cross, slots, load_sem,
):
    half = own.shape[1]
    loads = [
        pltpu.make_async_copy(block.at[EARLY : 2 * EARLY], raw.at[index], load_sem.at[index])
        for index, block in enumerate((beside, after, before))
    ]
    load_own = pltpu.make_async_copy(own, white, load_sem.at[3])
    load_early = pltpu.make_async_copy(early, blocks.at[0], load_sem.at[4])
    for load in loads + [load_own, load_early]:
        load.start()
    sums[...] = sums_in[...]
    counts[...] = jnp.zeros_like(counts)
    for index, load in enumerate(loads):
        load.wait()
        whiten(raw.at[index], rows, blocks.at[1, index], index == 0)
    load_own.wait()
    low = lax.rem(lax.axis_index("chan"), 2)
    counted = (lax.axis_index("off") == 0).astype(F32)
    even = (1 - low).astype(F32) * counted
    odd = low.astype(F32) * counted

    def own_rows(side):
        return lambda freq: white[side, freq].reshape(2 * CH, LANES)

    def late_pair(freq):
        return jnp.concatenate([blocks[1, 0, freq, 0], blocks[1, 1 + low, freq, 0]], axis=0)

    def both_halves(index, row):
        return lambda freq: jnp.concatenate([blocks[0, index, freq, row], blocks[1, index, freq, row]], axis=0)

    def beside_rows(freq):
        return jnp.concatenate([both_halves(0, 0)(freq), both_halves(0, 1)(freq)], axis=0)

    def late_labels():
        near = jnp.where(low == 0, labels[1, :, LANES:], as_integers(labels_beside[:, LANES:]))
        far = jnp.where(low == 0, labels[2, :, LANES:], as_integers(labels_before[1, :, LANES:]))
        return jnp.concatenate([near, far], axis=1)

    def moved_labels():
        return as_integers(jnp.where(low == 0, labels_beside[...].astype(F32), labels_before[0].astype(F32)))

    def other_labels():
        return jnp.where(low == 0, as_integers(labels_before[1, :, LANES:]), labels[2, :, LANES:])

    def add_to(side):
        def add(segment, values):
            sums[segment, side] += turned_back(values, side)

        return add

    cross_pairs(own_rows(low), late_pair, cross, half)
    add_bins(cross, late_labels, CH, even, slots, 2 * half, add_to(low), counts)
    cross_pairs(own_rows(1 - low), lambda freq: blocks[1, 2 - low, freq, 0], cross, half)
    add_bins(cross, other_labels, LANES, odd, slots, 2 * half, add_to(1 - low), counts)
    load_early.wait()
    cross_pairs(beside_rows, both_halves(1 + low, 0), cross, half)
    add_bins(cross, moved_labels, CH, even, slots, 2 * half, add_to(low), counts)


def reduce_kernel(
    sums, counts, self_tally, table, out, parts, near_in, far_out, far_in, near_send, near_recv, far_send, far_recv
):
    chan, off = lax.axis_index("chan"), lax.axis_index("off")
    low, high = lax.rem(chan, 2), lax.div(chan, 2)
    near = off * 2 + low

    def near_device(step):
        index = lax.rem(near + step, NEAR)
        return index, (high * 2 + lax.rem(index, 2), lax.div(index, 2))

    def far_device(step):
        index = lax.rem(high + step, FAR)
        return index, (index * 2 + low, off)

    barrier = pltpu.get_barrier_semaphore()

    def greet_near(step, _):
        pl.semaphore_signal(barrier, inc=1, device_id=near_device(step)[1], device_id_type=MESH)
        return 0

    def greet_far(step, _):
        pl.semaphore_signal(barrier, inc=1, device_id=far_device(step)[1], device_id_type=MESH)
        return 0

    lax.fori_loop(1, NEAR, greet_near, 0)
    lax.fori_loop(1, FAR, greet_far, 0)
    ones = jnp.ones((COUNT_ROWS, CH), F32)
    for segment in range(SEGMENTS):
        trace = lax.dot_general(
            sums[segment].reshape(table.shape[1], CLASSES),
            table[off],
            (((0,), (0,)), ((), ())),
            precision=lax.Precision.HIGHEST,
            preferred_element_type=F32,
        )
        tally = lax.dot_general(
            ones,
            counts[segment],
            (((1,), (1,)), ((), ())),
            precision=lax.Precision.HIGHEST,
            preferred_element_type=F32,
        )
        own = self_tally[segment : segment + 1, :] * (off == 0).astype(F32)
        tally = tally + jnp.broadcast_to(own, tally.shape)
        tally = jnp.concatenate([tally, jnp.zeros((COUNT_ROWS, LANES - CLASSES), F32)], axis=1)
        for part in range(2):
            parts[segment * 2 + part, :FAR, :] = trace[part * FAR : (part + 1) * FAR]
            parts[segment * 2 + part, FAR:, :] = tally
    pl.semaphore_wait(barrier, FAR - 1 + NEAR - 1)

    def near_copy(step):
        index, device = near_device(step)
        return pltpu.make_async_remote_copy(
            src_ref=parts.at[index],
            dst_ref=near_in.at[step - 1],
            send_sem=near_send.at[step - 1],
            recv_sem=near_recv.at[step - 1],
            device_id=device,
            device_id_type=MESH,
        )

    def far_copy(step):
        index, device = far_device(step)
        return pltpu.make_async_remote_copy(
            src_ref=far_out.at[index],
            dst_ref=far_in.at[step - 1],
            send_sem=far_send.at[step - 1],
            recv_sem=far_recv.at[step - 1],
            device_id=device,
            device_id_type=MESH,
        )

    def start_near(step, _):
        near_copy(step).start()
        return 0

    def start_far(step, _):
        far_copy(step).start()
        return 0

    lax.fori_loop(1, NEAR, start_near, 0)

    def add_near(step, total):
        near_copy(step).wait_recv()
        return total + near_in[step - 1]

    total = lax.fori_loop(1, NEAR, add_near, parts[near])
    for row in range(FAR):
        far_out[row] = jnp.concatenate([total[row : row + 1], total[FAR : FAR + 1]], axis=1)
    lax.fori_loop(1, FAR, start_far, 0)

    def add_far(step, total):
        far_copy(step).wait_recv()
        return total + far_in[step - 1]

    total = lax.fori_loop(1, FAR, add_far, far_out[high])
    lane = lax.broadcasted_iota(jnp.int32, (1, LANES), 1)
    count = jnp.sum(jnp.where(lane == low * FAR + high, total[:, LANES:], 0.0), axis=1, keepdims=True)
    out[...] = total[:, :LANES] / jnp.sqrt(jnp.maximum(count, 1.0))

    def end_near(step, _):
        near_copy(step).wait_send()
        return 0

    def end_far(step, _):
        far_copy(step).wait_send()
        return 0

    lax.fori_loop(1, NEAR, end_near, 0)
    lax.fori_loop(1, FAR, end_far, 0)


def lag_tables(groups, freqs, lags):
    nfreq = groups * freqs
    shifts = np.arange(lags) - lags // 2
    theta = math.pi * np.mod(np.arange(nfreq)[:, None] * shifts[None, :], 2 * nfreq) / nfreq
    table = np.stack([np.cos(theta), -np.sin(theta)]).reshape(2, groups, 2, freqs // 2, lags)
    table = table.transpose(1, 2, 0, 3, 4).reshape(groups, 2 * freqs, lags)
    return jnp.asarray((table / HALF).astype(np.float32))


def on_device(spectra, pair_bins):
    freqs = spectra.shape[1]
    half = freqs // 2
    vmem_limit = 56 * 1024 * 1024
    white_shape = jax.ShapeDtypeStruct((2, half, 2, CH, LANES), BF16)
    early_shape = jax.ShapeDtypeStruct((3, half, 2, EARLY, LANES), BF16)
    block_shape = jax.ShapeDtypeStruct((CH, half, LANES), BF16)
    sums_shape = jax.ShapeDtypeStruct((SEGMENTS, 2, 2 * half, CLASSES), F32)
    counts_shape = jax.ShapeDtypeStruct((SEGMENTS, CLASSES, CH), F32)
    square = pltpu.VMEM((CH, CH), F32)

    after, before, beside, white, early, labels_before, labels_beside, sums, tally = pl.pallas_call(
        exchange_kernel,
        out_shape=[
            block_shape,
            block_shape,
            block_shape,
            white_shape,
            early_shape,
            jax.ShapeDtypeStruct((2, CH, CH), BF16),
            jax.ShapeDtypeStruct((CH, CH), BF16),
            sums_shape,
            jax.ShapeDtypeStruct((16, CLASSES), F32),
        ],
        in_specs=[ANY] * 2,
        out_specs=[ANY] * 5 + [VMEM] * 4,
        scratch_shapes=[
            pltpu.VMEM(spectra.shape, BF16),
            pltpu.VMEM((3, EARLY, half, LANES), BF16),
            pltpu.VMEM(pair_bins.shape[1:], jnp.int32),
            pltpu.VMEM((3, CH, CH), BF16),
            pltpu.VMEM(white_shape.shape, BF16),
            pltpu.VMEM(early_shape.shape, BF16),
            pltpu.VMEM((CH * (freqs + PAD), LANES), F32),
            pltpu.VMEM((2, 2 * freqs * (CH + PAD), LANES), F32),
            square,
            square,
            DMA((7,)),
            DMA((9,)),
            DMA((9,)),
        ],
        compiler_params=pltpu.CompilerParams(
            collective_id=1, has_side_effects=True, vmem_limit_bytes=vmem_limit
        ),
    )(spectra, pair_bins)
    sums, counts = pl.pallas_call(
        pairs_kernel,
        out_shape=[sums_shape, counts_shape],
        in_specs=[ANY] * 5 + [VMEM] * 4,
        out_specs=[VMEM] * 2,
        scratch_shapes=[
            pltpu.VMEM(white_shape.shape, BF16),
            pltpu.VMEM((2,) + early_shape.shape, BF16),
            pltpu.VMEM((3, EARLY, half, LANES), BF16),
            pltpu.VMEM((EARLY * (half + PAD), LANES), F32),
            pltpu.VMEM((2, 2 * half * (CH + PAD), LANES), F32),
            square,
            DMA((5,)),
        ],
        compiler_params=pltpu.CompilerParams(vmem_limit_bytes=vmem_limit),
    )(white, early, beside, after, before, pair_bins[0], labels_beside, labels_before, sums)
    return pl.pallas_call(
        reduce_kernel,
        out_shape=jax.ShapeDtypeStruct((1, LANES), F32),
        in_specs=[VMEM] * 4,
        out_specs=VMEM,
        scratch_shapes=[
            pltpu.VMEM((NEAR, FAR + COUNT_ROWS, LANES), F32),
            pltpu.VMEM((NEAR - 1, FAR + COUNT_ROWS, LANES), F32),
            pltpu.VMEM((FAR, 1, 2 * LANES), F32),
            pltpu.VMEM((FAR - 1, 1, 2 * LANES), F32),
            DMA((NEAR - 1,)),
            DMA((NEAR - 1,)),
            DMA((FAR - 1,)),
            DMA((FAR - 1,)),
        ],
        compiler_params=pltpu.CompilerParams(collective_id=0, has_side_effects=True),
    )(sums, counts, tally, lag_tables(lax.axis_size("off"), freqs, LANES))


def solution(mesh):
    in_specs = (P("chan", "off", None), P("chan", None, None, None))
    out_specs = P(("chan", "off"), None)
    return jax.shard_map(
        on_device, mesh=mesh, in_specs=in_specs, out_specs=out_specs, check_vma=False
    )
```

time: 86.8 us -> 88.1 us (1.015)
  Pallas kernels: 85.4 us -> 86.7 us
    pallas_call x1, Pallas kernels: 27.7 us -> 18.7 us  [on_device(): pl.pallas_call(pairs_kernel, out_shape=[sums_shape, counts_shape], in_spe...]
    pallas_call x1, Pallas kernels: 18.4 us -> 25.6 us  [on_device(): pl.pallas_call(reduce_kernel, out_shape=jax.ShapeDtypeStruct((1, LANES),...]
    pallas_call x1, Pallas kernels: 39.3 us -> 42.4 us  [on_device(): pl.pallas_call(exchange_kernel, out_shape=[block_shape, block_shape, bloc...]
where the time goes in v4:
time: 88.1 us; the launch traced here: 87.9 us
  Pallas kernels  86.7 us (98%)
  local copies, waits for them, and re-layouts  1.14 us (1%)
    pallas_call x1, Pallas kernels, on_device(): pl.pallas_call(exchange_kernel, out_shape=[block_shape, block_shape, bloc...  42.4 us
    pallas_call x1, Pallas kernels, on_device(): pl.pallas_call(reduce_kernel, out_shape=jax.ShapeDtypeStruct((1, LANES),...  25.6 us
    pallas_call x1, Pallas kernels, on_device(): pl.pallas_call(pairs_kernel, out_shape=[sums_shape, counts_shape], in_spe...  18.7 us

profile of v4, /device:TPU:1, one launch (start us, length us, event | category | flops | bytes accessed | tf_op | source)
XLA Modules:
  0.0 87.9 jit_solution(14162618048159321219)
XLA Ops:
  0.0 42.4 %shard_map.37 = (bf16[256,16,128]{2,1,0:T(8,128)(2,1)}, bf16[256,16,128]{2,1,0:T(8,128)(2,1)}, bf16[256,16,128]{2,1,0:T(8,128)(2,1)}, bf16[2,16,2,256,128]{4,3,2...) custom-call(bf16[256,32,128]{2,1,0:T(8,128)(2,1)} %spectra.1, ...), custom_call_target="tpu_custom_call" | custom-call | tf_op jit(solution)/shard_map/pallas_call | solution.py:535
  42.4 18.7 %shard_map.38 = (f32[4,2,32,64]{3,2,1,0:T(8,128)}, f32[4,64,256]{2,1,0:T(8,128)}) custom-call(bf16[2,16,2,256,128]{4,3,2,1,0:T(8,128)(2,1)} %get-tuple-element.16.own, bf16[3,16,2,128,128]{4,3,2,1,0:T(8,128)(2,1)} %get-tuple-element.17.early, bf16[256,16,128]{2,1,0:T(8,128)(2,1)} %get-tuple-element.18.beside, bf16[256,16,128]{2,1,0:T(8,128)(2,1)} %get-tuple-element.19.after, ...), custom_call_target="tpu_custom_call" | custom-call | tf_op jit(solution)/shard_map/pallas_call | solution.py:569
  61.1 25.6 %shard_map.39 = f32[1,128]{1,0:T(1,128)} custom-call(f32[4,2,32,64]{3,2,1,0:T(8,128)} %get-tuple-element.24.sums, f32[4,64,256]{2,1,0:T(8,128)} %get-tuple-element.25.counts, f32[16,64]{1,0:T(8,128)} %get-tuple-element.26.self_tally, f32[4,64,128]{2,1,0:T(8,128)} %constant.2.clone.table), custom_call_target="tpu_custom_call" | custom-call | tf_op jit(solution)/shard_map/pallas_call | solution.py:585
  86.7 1.1 %copy.5 = f32[1,128]{1,0:T(1,128)} copy(f32[1,128]{1,0:T(1,128)} %shard_map.39) | data formatting | bytes 1024

commit v5 on v4

--- a/solution.py
+++ b/solution.py
@@ -27,7 +27,7 @@
 FAR = 32
 FREQ_UNROLL = 8
 ROW_UNROLL = 64
-SELF_UNROLL = 32
+STATIC_UNROLL = 64
 COUNT_ROWS = 8
 
 
@@ -81,8 +81,8 @@
     lax.fori_loop(0, freqs // FREQ_UNROLL, body, 0)
 
 
-def slot_numbers(width):
-    shape = (CLASSES // 16, 16, width)
+def slot_numbers(width, count=CLASSES):
+    shape = (count // 16, 16, width)
     ids = lax.broadcasted_iota(jnp.int32, shape, 0) * 16 + lax.broadcasted_iota(jnp.int32, shape, 1)
     return ids.astype(F32).astype(BF16)
 
@@ -92,16 +92,17 @@
     return ((classes & 1) * (CLASSES // 2) + lax.shift_right_logical(classes, 1)).astype(F32)
 
 
-def piece_of(cross, i, nrows, width):
-    sides = [cross[side, pl.ds(i, nrows, stride=CH + PAD), :] for side in range(width // LANES)]
-    return jnp.concatenate(sides, axis=1).astype(BF16)
+def piece_of(cross, i, nrows, sides):
+    pieces = [cross[side, pl.ds(i, nrows, stride=CH + PAD), :] for side in sides]
+    return jnp.concatenate(pieces, axis=1).astype(BF16)
 
 
 def row_of(ref, i, width):
     return jnp.broadcast_to(ref[pl.ds(i, 1), :][:, :width], (16, width)).astype(BF16)
 
 
-def add_bins(cross, read_labels, width, weight, slots, nrows, add_sums, counts):
+def add_bins(cross, read_labels, sides, weight, slots, nrows, add_sums, counts):
+    width = len(sides) * LANES
     slot_ids = slot_numbers(width)
     unroll = ROW_UNROLL * CH // width
     one = jnp.ones((), BF16)
@@ -118,7 +119,7 @@
             tally = None
             for part in range(unroll):
                 i = block * unroll + part
-                pieces.append(piece_of(cross, i, nrows, width))
+                pieces.append(piece_of(cross, i, nrows, sides))
                 row = row_of(slots, i, width)
                 onehot = jnp.where(row[None] == slot_ids, one, zero).reshape(CLASSES, width)
                 onehots.append(onehot)
@@ -141,9 +142,20 @@
     lax.fori_loop(first, last + 1, add_segment, 0)
 
 
-def add_all_bins(cross, slots, segments, width, nrows, add_sums, add_tally, begin=0, end=CH):
-    slot_ids = slot_numbers(width)
-    unroll = SELF_UNROLL * CH // width
+def place_marks(marks, masks, slots, segments):
+    width = marks.shape[1]
+    groups = SEGMENTS // masks
+    segment = marks & (SEGMENTS - 1)
+    slots[:, :width] = slots_of(marks) + (CLASSES * (segment & (groups - 1))).astype(F32)
+    segments[:, :width] = lax.shift_right_logical(segment, groups // 2).astype(F32)
+
+
+def add_all_bins(cross, slots, segments, masks, sides, nrows, add_sums, add_tally, begin=0, end=CH):
+    width = len(sides) * LANES
+    groups = SEGMENTS // masks
+    nslots = groups * CLASSES
+    slot_ids = slot_numbers(width, nslots)
+    unroll = STATIC_UNROLL
     row_ids = lax.broadcasted_iota(jnp.int32, (16, width), 0).astype(F32).astype(BF16)
     one = jnp.ones((), BF16)
     zero = jnp.zeros((), BF16)
@@ -152,16 +164,16 @@
         pieces, onehots = [], []
         for part in range(unroll):
             i = block * unroll + part
-            values = piece_of(cross, i, nrows, width).reshape(nrows // 16, 16, width)
+            values = piece_of(cross, i, nrows, sides).reshape(nrows // 16, 16, width)
             place = row_of(segments, i, width)
             masked = [
-                jnp.where(place[None] == jnp.full((), segment, BF16), values, zero).reshape(nrows, width)
-                for segment in range(SEGMENTS)
+                jnp.where(place[None] == jnp.full((), mask, BF16), values, zero).reshape(nrows, width)
+                for mask in range(masks)
             ]
             masked.append(jnp.where(place == row_ids, one, zero))
             pieces.append(jnp.concatenate(masked, axis=0))
             row = row_of(slots, i, width)
-            onehots.append(jnp.where(row[None] == slot_ids, one, zero).reshape(CLASSES, width))
+            onehots.append(jnp.where(row[None] == slot_ids, one, zero).reshape(nslots, width))
         binned = lax.dot_general(
             jnp.concatenate(pieces, axis=1),
             jnp.concatenate(onehots, axis=1),
@@ -169,8 +181,11 @@
             preferred_element_type=F32,
         )
         for segment in range(SEGMENTS):
-            add_sums(segment, binned[segment * nrows : (segment + 1) * nrows])
-        add_tally(binned[SEGMENTS * nrows :])
+            mask, group = segment // groups, segment % groups
+            columns = slice(group * CLASSES, (group + 1) * CLASSES)
+            tally_row = masks * nrows + mask
+            add_sums(segment, binned[mask * nrows : (mask + 1) * nrows, columns])
+            add_tally(segment, binned[tally_row : tally_row + 1, columns])
         return 0
 
     lax.fori_loop(begin // unroll, end // unroll, add_rows, 0)
@@ -248,9 +263,7 @@
     def _():
         near_copy.start()
 
-    marks = labels[0]
-    slots[...] = slots_of(marks)
-    segments[...] = (marks & (SEGMENTS - 1)).astype(F32)
+    place_marks(labels[0], 2, slots, segments)
     sums[...] = jnp.zeros_like(sums)
     tally[...] = jnp.zeros_like(tally)
     load_raw.wait()
@@ -268,13 +281,13 @@
         sums[segment] += values.reshape(2, 2 * half, CLASSES)
 
     def add_tally(weight):
-        def add(values):
-            tally[...] += values * weight
+        def add(segment, values):
+            tally[segment : segment + 1, :] += values * weight
 
         return add
 
     bin_self = functools.partial(
-        add_all_bins, cross, slots, segments, CH, 4 * half, add_self, add_tally(1.0)
+        add_all_bins, cross, slots, segments, 2, (0, 1), 4 * half, add_self, add_tally(1.0)
     )
     bin_self(begin=0, end=CH // 2)
     for copy in copies[1]:
@@ -303,8 +316,7 @@
         ],
         axis=1,
     )
-    slots[...] = slots_of(marks)
-    segments[...] = (marks & (SEGMENTS - 1)).astype(F32)
+    place_marks(marks, SEGMENTS, slots, segments)
 
     def add_to(side):
         def add(segment, values):
@@ -318,12 +330,11 @@
         cross,
         half,
     )
-    add_all_bins(cross, slots, segments, CH, 2 * half, add_to(low), add_tally(even))
+    add_all_bins(cross, slots, segments, SEGMENTS, (0, 1), 2 * half, add_to(low), add_tally(even))
     marks = jnp.where(low == 0, before_far, own_far)[:, :LANES]
-    slots[:, :LANES] = slots_of(marks)
-    segments[:, :LANES] = (marks & (SEGMENTS - 1)).astype(F32)
+    place_marks(marks, SEGMENTS, slots, segments)
     cross_pairs(own(1 - low), lambda freq: early[2 - low, freq, 0], cross, half)
-    add_all_bins(cross, slots, segments, LANES, 2 * half, add_to(1 - low), add_tally(odd))
+    add_all_bins(cross, slots, segments, SEGMENTS, (0,), 2 * half, add_to(1 - low), add_tally(odd))
 
     keep.wait()
     keep_early.wait()
@@ -373,10 +384,11 @@
     def beside_rows(freq):
         return jnp.concatenate([both_halves(0, 0)(freq), both_halves(0, 1)(freq)], axis=0)
 
-    def late_labels():
-        near = jnp.where(low == 0, labels[1, :, LANES:], as_integers(labels_beside[:, LANES:]))
-        far = jnp.where(low == 0, labels[2, :, LANES:], as_integers(labels_before[1, :, LANES:]))
-        return jnp.concatenate([near, far], axis=1)
+    def near_labels():
+        return jnp.where(low == 0, labels[1, :, LANES:], as_integers(labels_beside[:, LANES:]))
+
+    def far_labels():
+        return jnp.where(low == 0, labels[2, :, LANES:], as_integers(labels_before[1, :, LANES:]))
 
     def moved_labels():
         return as_integers(jnp.where(low == 0, labels_beside[...].astype(F32), labels_before[0].astype(F32)))
@@ -391,12 +403,13 @@
         return add
 
     cross_pairs(own_rows(low), late_pair, cross, half)
-    add_bins(cross, late_labels, CH, even, slots, 2 * half, add_to(low), counts)
+    add_bins(cross, near_labels, (0,), even, slots, 2 * half, add_to(low), counts)
+    add_bins(cross, far_labels, (1,), even, slots, 2 * half, add_to(low), counts)
     cross_pairs(own_rows(1 - low), lambda freq: blocks[1, 2 - low, freq, 0], cross, half)
-    add_bins(cross, other_labels, LANES, odd, slots, 2 * half, add_to(1 - low), counts)
+    add_bins(cross, other_labels, (0,), odd, slots, 2 * half, add_to(1 - low), counts)
     load_early.wait()
     cross_pairs(beside_rows, both_halves(1 + low, 0), cross, half)
-    add_bins(cross, moved_labels, CH, even, slots, 2 * half, add_to(low), counts)
+    add_bins(cross, moved_labels, (0, 1), even, slots, 2 * half, add_to(low), counts)
 
 
 def reduce_kernel(

time: 88.1 us -> 77.8 us (0.88)
  Pallas kernels: 86.7 us -> 76.4 us
    pallas_call x1, Pallas kernels: 25.6 us -> 19.9 us  [on_device(): pl.pallas_call(reduce_kernel, out_shape=jax.ShapeDtypeStruct((1, LANES),...]
    pallas_call x1, Pallas kernels: 42.4 us -> 37.6 us  [on_device(): pl.pallas_call(exchange_kernel, out_shape=[block_shape, block_shape, bloc...]
where the time goes in v5:
time: 77.8 us; the launch traced here: 77.6 us
  Pallas kernels  76.4 us (98%)
  local copies, waits for them, and re-layouts  1.14 us (1%)
    pallas_call x1, Pallas kernels, on_device(): pl.pallas_call(exchange_kernel, out_shape=[block_shape, block_shape, bloc...  37.6 us
    pallas_call x1, Pallas kernels, on_device(): pl.pallas_call(reduce_kernel, out_shape=jax.ShapeDtypeStruct((1, LANES),...  19.9 us
    pallas_call x1, Pallas kernels, on_device(): pl.pallas_call(pairs_kernel, out_shape=[sums_shape, counts_shape], in_spe...  18.9 us

profile of v5, /device:TPU:1, one launch (start us, length us, event | category | flops | bytes accessed | tf_op | source)
XLA Modules:
  0.0 77.6 jit_solution(848973426859981942)
XLA Ops:
  0.0 37.6 %shard_map.37 = (bf16[256,16,128]{2,1,0:T(8,128)(2,1)}, bf16[256,16,128]{2,1,0:T(8,128)(2,1)}, bf16[256,16,128]{2,1,0:T(8,128)(2,1)}, bf16[2,16,2,256,128]{4,3,2...) custom-call(bf16[256,32,128]{2,1,0:T(8,128)(2,1)} %spectra.1, ...), custom_call_target="tpu_custom_call" | custom-call | tf_op jit(solution)/shard_map/pallas_call | solution.py:548
  37.6 18.9 %shard_map.38 = (f32[4,2,32,64]{3,2,1,0:T(8,128)}, f32[4,64,256]{2,1,0:T(8,128)}) custom-call(bf16[2,16,2,256,128]{4,3,2,1,0:T(8,128)(2,1)} %get-tuple-element.16.own, bf16[3,16,2,128,128]{4,3,2,1,0:T(8,128)(2,1)} %get-tuple-element.17.early, bf16[256,16,128]{2,1,0:T(8,128)(2,1)} %get-tuple-element.18.beside, bf16[256,16,128]{2,1,0:T(8,128)(2,1)} %get-tuple-element.19.after, ...), custom_call_target="tpu_custom_call" | custom-call | tf_op jit(solution)/shard_map/pallas_call | solution.py:582
  56.6 19.9 %shard_map.39 = f32[1,128]{1,0:T(1,128)} custom-call(f32[4,2,32,64]{3,2,1,0:T(8,128)} %get-tuple-element.24.sums, f32[4,64,256]{2,1,0:T(8,128)} %get-tuple-element.25.counts, f32[16,64]{1,0:T(8,128)} %get-tuple-element.26.self_tally, f32[4,64,128]{2,1,0:T(8,128)} %constant.2.clone.table), custom_call_target="tpu_custom_call" | custom-call | tf_op jit(solution)/shard_map/pallas_call | solution.py:598
  76.4 1.1 %copy.5 = f32[1,128]{1,0:T(1,128)} copy(f32[1,128]{1,0:T(1,128)} %shard_map.39) | data formatting | bytes 1024

commit v6 on v1

v6 whole, which is shorter than its diff:
```python
import functools
import math

import jax
import jax.numpy as jnp
import numpy as np
from jax import lax
from jax.experimental import pallas as pl
from jax.experimental.pallas import tpu as pltpu
from jax.sharding import PartitionSpec as P

F32 = jnp.float32
BF16 = jnp.bfloat16
MESH = pl.DeviceIdType.MESH
VMEM = pl.BlockSpec(memory_space=pltpu.VMEM)
ANY = pl.BlockSpec(memory_space=pl.ANY)
DMA = pltpu.SemaphoreType.DMA

CH = 256
LANES = 128
EARLY = CH // 2
HALF = LANES // 2
SEGMENTS = 4
CLASSES = 64
PAD = 8
NEAR = 8
FAR = 32
FREQ_UNROLL = 8
STATIC_UNROLL = 64
COUNT_ROWS = 8


def whiten(raw, rows, white, with_rotated):
    channels, freqs, _ = raw.shape
    step = freqs + PAD
    chunk = 32

    def normalise(block, _):
        values = raw[pl.ds(block * chunk, chunk)].astype(F32)
        meansq = jnp.mean(values * values, axis=-1, keepdims=True)
        scaled = values * lax.rsqrt(meansq + 1e-05)
        for channel in range(chunk):
            start = pl.multiple_of((block * chunk + channel) * step, 8)
            rows[pl.ds(start, freqs), :] = scaled[channel]
        return 0

    lax.fori_loop(0, channels // chunk, normalise, 0)

    def regroup(block, _):
        for part in range(FREQ_UNROLL):
            freq = block * FREQ_UNROLL + part
            values = rows[pl.ds(freq, channels, stride=step), :]
            white[freq, 0] = values.astype(BF16)
            if with_rotated:
                lane = lax.broadcasted_iota(jnp.int32, (channels, LANES), 1)
                turned = pltpu.roll(values, HALF, 1)
                white[freq, 1] = jnp.where(lane < HALF, turned, -turned).astype(BF16)
        return 0

    lax.fori_loop(0, freqs // FREQ_UNROLL, regroup, 0)


def cross_pairs(first, second, cross, freqs, top=0):
    step = CH + PAD

    def body(block, _):
        for part in range(FREQ_UNROLL):
            freq = block * FREQ_UNROLL + part
            product = lax.dot_general(
                first(freq), second(freq), (((1,), (1,)), ((), ())), preferred_element_type=F32
            )
            for row in range(2):
                start = pl.multiple_of((top + freq + row * freqs) * step, 8)
                for side in range(product.shape[1] // LANES):
                    cross[side, pl.ds(start, CH), :] = product[
                        row * CH : (row + 1) * CH, side * LANES : (side + 1) * LANES
                    ]
        return 0

    lax.fori_loop(0, freqs // FREQ_UNROLL, body, 0)


def slot_numbers(width, count=CLASSES):
    shape = (count // 16, 16, width)
    ids = lax.broadcasted_iota(jnp.int32, shape, 0) * 16 + lax.broadcasted_iota(jnp.int32, shape, 1)
    return ids.astype(F32).astype(BF16)


def slots_of(marks):
    classes = lax.shift_right_logical(marks, 2)
    return ((classes & 1) * (CLASSES // 2) + lax.shift_right_logical(classes, 1)).astype(F32)


def piece_of(cross, i, nrows, sides):
    pieces = [cross[side, pl.ds(i, nrows, stride=CH + PAD), :] for side in sides]
    return jnp.concatenate(pieces, axis=1).astype(BF16)


def row_of(ref, i, width):
    return jnp.broadcast_to(ref[pl.ds(i, 1), :][:, :width], (16, width)).astype(BF16)


def place_marks(marks, masks, slots, segments):
    width = marks.shape[1]
    groups = SEGMENTS // masks
    segment = marks & (SEGMENTS - 1)
    slots[:, :width] = slots_of(marks) + (CLASSES * (segment & (groups - 1))).astype(F32)
    segments[:, :width] = lax.shift_right_logical(segment, groups // 2).astype(F32)


def add_all_bins(cross, slots, segments, masks, sides, nrows, add_sums, add_tally, begin=0, end=CH):
    width = len(sides) * LANES
    groups = SEGMENTS // masks
    nslots = groups * CLASSES
    slot_ids = slot_numbers(width, nslots)
    unroll = STATIC_UNROLL
    row_ids = lax.broadcasted_iota(jnp.int32, (16, width), 0).astype(F32).astype(BF16)
    one = jnp.ones((), BF16)
    zero = jnp.zeros((), BF16)

    def add_rows(block, _):
        pieces, onehots = [], []
        for part in range(unroll):
            i = block * unroll + part
            values = piece_of(cross, i, nrows, sides).reshape(nrows // 16, 16, width)
            place = row_of(segments, i, width)
            masked = [
                jnp.where(place[None] == jnp.full((), mask, BF16), values, zero).reshape(nrows, width)
                for mask in range(masks)
            ]
            masked.append(jnp.where(place == row_ids, one, zero))
            pieces.append(jnp.concatenate(masked, axis=0))
            row = row_of(slots, i, width)
            onehots.append(jnp.where(row[None] == slot_ids, one, zero).reshape(nslots, width))
        binned = lax.dot_general(
            jnp.concatenate(pieces, axis=1),
            jnp.concatenate(onehots, axis=1),
            (((1,), (1,)), ((), ())),
            preferred_element_type=F32,
        )
        for segment in range(SEGMENTS):
            mask, group = segment // groups, segment % groups
            columns = slice(group * CLASSES, (group + 1) * CLASSES)
            tally_row = masks * nrows + mask
            add_sums(segment, binned[mask * nrows : (mask + 1) * nrows, columns])
            add_tally(segment, binned[tally_row : tally_row + 1, columns])
        return 0

    lax.fori_loop(begin // unroll, end // unroll, add_rows, 0)


def as_integers(values):
    return values.astype(F32).astype(jnp.int32)


def network_kernel(
    spectra, pair_bins, table, out,
    raw, across_raw, beside_raw, labels, sent_labels, across_labels, beside_labels, white, across, beside,
    rows, cross, slots, segments, sums, tally, parts, near_in, far_out, far_in,
    local_sem, send_sem, recv_sem, near_send, near_recv, far_send, far_recv,
):
    freqs = raw.shape[1]
    chan, off = lax.axis_index("chan"), lax.axis_index("off")
    count = lax.axis_size("chan")
    low, high = lax.rem(chan, 2), lax.div(chan, 2)
    core = lax.rem(off, 2)
    heavy = low == core
    light = low != core
    near = off * 2 + low
    target = lax.rem(chan + count - 2 + 4 * core, count)
    partner = chan + 1 - 2 * low

    def near_device(step):
        index = lax.rem(near + step, NEAR)
        return index, (high * 2 + lax.rem(index, 2), lax.div(index, 2))

    def far_device(step):
        index = lax.rem(high + step, FAR)
        return index, (index * 2 + low, off)

    load_labels = pltpu.make_async_copy(pair_bins.at[0], labels, local_sem.at[0])
    load_raw = pltpu.make_async_copy(spectra, raw, local_sem.at[1])
    load_labels.start()
    load_raw.start()
    barrier = pltpu.get_barrier_semaphore()

    def greet_near(step, _):
        pl.semaphore_signal(barrier, inc=1, device_id=near_device(step)[1], device_id_type=MESH)
        return 0

    def greet_far(step, _):
        pl.semaphore_signal(barrier, inc=1, device_id=far_device(step)[1], device_id_type=MESH)
        return 0

    lax.fori_loop(1, FAR, greet_far, 0)
    lax.fori_loop(1, NEAR, greet_near, 0)
    load_labels.wait()
    one_ahead, two_ahead = labels[1].astype(F32), labels[2].astype(F32)
    one_turned = one_ahead.T
    sent_labels[0] = one_turned.astype(BF16)
    sent_labels[1] = two_ahead.T.astype(BF16)
    sent_labels[2] = jnp.where(core == 0, one_ahead, one_turned).astype(BF16)

    @pl.when(core == 0)
    def _():
        across_labels[0] = one_ahead.astype(BF16)
        across_labels[1] = two_ahead.astype(BF16)

    pl.semaphore_wait(barrier, FAR - 1 + NEAR - 1)

    def remote(index, source, landing, chan_to):
        return pltpu.make_async_remote_copy(
            src_ref=source,
            dst_ref=landing,
            send_sem=send_sem.at[index],
            recv_sem=recv_sem.at[index],
            device_id=(chan_to, off),
            device_id_type=MESH,
        )

    pieces = [slice(piece * EARLY, (piece + 1) * EARLY) for piece in range(2)]
    across_copies = [remote(i, spectra.at[part], across_raw.at[part], target) for i, part in enumerate(pieces)]
    beside_copies = [remote(2 + i, spectra.at[part], beside_raw.at[part], partner) for i, part in enumerate(pieces)]
    beside_copies.append(remote(4, sent_labels.at[2], beside_labels, partner))
    two_copy = remote(5, sent_labels.at[1], across_labels.at[1], target)
    one_copy = remote(6, sent_labels.at[0], across_labels.at[0], target)
    across_copies[0].start()

    @pl.when(light)
    def _():
        beside_copies[0].start()
        beside_copies[2].start()

    @pl.when(core == 1)
    def _():
        two_copy.start()

    @pl.when(jnp.logical_and(core == 1, low == 1))
    def _():
        one_copy.start()

    place_marks(labels[0], 2, slots, segments)
    sums[...] = jnp.zeros_like(sums)
    tally[...] = jnp.zeros_like(tally)
    load_raw.wait()
    whiten(raw, rows, white, True)

    def own(freq):
        return white[freq].reshape(2 * CH, LANES)

    def add_tally(segment, values):
        tally[segment : segment + 1, :] += values

    def add_self(segment, values):
        sums[segment] += values

    sign = (1 - 2 * core).astype(F32)

    def add_pairs(segment, values):
        sums[segment, :freqs] += values[:freqs]
        sums[segment, freqs:] += values[freqs:] * sign

    def bin_pairs(marks):
        place_marks(marks, 2, slots, segments)
        add_all_bins(cross, slots, segments, 2, (0, 1), 2 * freqs, add_pairs, add_tally)

    cross_pairs(own, lambda freq: white[freq, 0], cross, freqs)
    bin_self = functools.partial(
        add_all_bins, cross, slots, segments, 2, (0, 1), 2 * freqs, add_self, add_tally
    )
    bin_self(begin=0, end=CH // 2)
    across_copies[1].start()

    @pl.when(light)
    def _():
        beside_copies[1].start()

    bin_self(begin=CH // 2, end=CH)
    across_copies[0].wait_recv()
    whiten(across_raw.at[pieces[0]], rows, across.at[0], False)

    @pl.when(core == 1)
    def _():
        two_copy.wait_recv()

    def beside_marks():
        return jnp.where(core == 0, labels[1], as_integers(beside_labels[...]))

    def half_marks(piece):
        lanes = slice(piece * LANES, (piece + 1) * LANES)
        return jnp.concatenate([beside_marks()[:, lanes], as_integers(across_labels[1])[:, lanes]], axis=1)

    def half_blocks(piece):
        return lambda freq: jnp.concatenate([beside[piece, freq, 0], across[piece, freq, 0]], axis=0)

    def whole(block, row):
        return lambda freq: jnp.concatenate([block[0, freq, row], block[1, freq, row]], axis=0)

    def beside_rows(freq):
        return jnp.concatenate([whole(beside, 0)(freq), whole(beside, 1)(freq)], axis=0)

    @pl.when(heavy)
    def _():
        beside_copies[0].wait_recv()
        beside_copies[2].wait_recv()
        whiten(beside_raw.at[pieces[0]], rows, beside.at[0], True)
        cross_pairs(own, half_blocks(0), cross, freqs)
        bin_pairs(half_marks(0))

    across_copies[1].wait_recv()
    whiten(across_raw.at[pieces[1]], rows, across.at[1], False)

    @pl.when(heavy)
    def _():
        beside_copies[1].wait_recv()
        whiten(beside_raw.at[pieces[1]], rows, beside.at[1], True)
        cross_pairs(own, half_blocks(1), cross, freqs)
        bin_pairs(half_marks(1))

        @pl.when(core == 1)
        def _():
            one_copy.wait_recv()

        cross_pairs(beside_rows, whole(across, 0), cross, freqs)
        bin_pairs(as_integers(jnp.where(core == 0, beside_labels[...].astype(F32), across_labels[0].astype(F32))))

    @pl.when(light)
    def _():
        cross_pairs(own, whole(across, 0), cross, freqs)
        bin_pairs(as_integers(across_labels[1]))

    counted = (off == 0).astype(F32)
    for segment in range(SEGMENTS):
        trace = lax.dot_general(
            sums[segment],
            table[off],
            (((0,), (0,)), ((), ())),
            precision=lax.Precision.HIGHEST,
            preferred_element_type=F32,
        )
        counts = jnp.broadcast_to(tally[segment : segment + 1, :] * counted, (COUNT_ROWS, CLASSES))
        counts = jnp.concatenate([counts, jnp.zeros((COUNT_ROWS, LANES - CLASSES), F32)], axis=1)
        for part in range(2):
            parts[segment * 2 + part, :FAR, :] = trace[part * FAR : (part + 1) * FAR]
            parts[segment * 2 + part, FAR:, :] = counts

    def near_copy(step):
        index, device = near_device(step)
        return pltpu.make_async_remote_copy(
            src_ref=parts.at[index],
            dst_ref=near_in.at[step - 1],
            send_sem=near_send.at[step - 1],
            recv_sem=near_recv.at[step - 1],
            device_id=device,
            device_id_type=MESH,
        )

    def far_copy(step):
        index, device = far_device(step)
        return pltpu.make_async_remote_copy(
            src_ref=far_out.at[index],
            dst_ref=far_in.at[step - 1],
            send_sem=far_send.at[step - 1],
            recv_sem=far_recv.at[step - 1],
            device_id=device,
            device_id_type=MESH,
        )

    def start_near(step, _):
        near_copy(step).start()
        return 0

    def start_far(step, _):
        far_copy(step).start()
        return 0

    lax.fori_loop(1, NEAR, start_near, 0)

    def add_near(step, total):
        near_copy(step).wait_recv()
        return total + near_in[step - 1]

    total = lax.fori_loop(1, NEAR, add_near, parts[near])
    for row in range(FAR):
        far_out[row] = jnp.concatenate([total[row : row + 1], total[FAR : FAR + 1]], axis=1)
    lax.fori_loop(1, FAR, start_far, 0)

    def add_far(step, total):
        far_copy(step).wait_recv()
        return total + far_in[step - 1]

    total = lax.fori_loop(1, FAR, add_far, far_out[high])
    lane = lax.broadcasted_iota(jnp.int32, (1, LANES), 1)
    pairs = jnp.sum(jnp.where(lane == low * FAR + high, total[:, LANES:], 0.0), axis=1, keepdims=True)
    out[...] = total[:, :LANES] / jnp.sqrt(jnp.maximum(pairs, 1.0))

    def end_near(step, _):
        near_copy(step).wait_send()
        return 0

    def end_far(step, _):
        far_copy(step).wait_send()
        return 0

    lax.fori_loop(1, NEAR, end_near, 0)
    lax.fori_loop(1, FAR, end_far, 0)
    for copy in across_copies:
        copy.wait_send()

    @pl.when(light)
    def _():
        for copy in beside_copies:
            copy.wait_send()

    @pl.when(core == 1)
    def _():
        two_copy.wait_send()

    @pl.when(jnp.logical_and(core == 1, low == 1))
    def _():
        one_copy.wait_send()


def lag_tables(groups, freqs, lags):
    nfreq = groups * freqs
    shifts = np.arange(lags) - lags // 2
    theta = math.pi * np.mod(np.arange(nfreq)[:, None] * shifts[None, :], 2 * nfreq) / nfreq
    table = np.stack([np.cos(theta), -np.sin(theta)]).reshape(2, groups, freqs, lags)
    table = table.transpose(1, 0, 2, 3).reshape(groups, 2 * freqs, lags)
    return jnp.asarray((table / HALF).astype(np.float32))


def on_device(spectra, pair_bins):
    freqs = spectra.shape[1]
    block = pltpu.VMEM(spectra.shape, BF16)
    square = pltpu.VMEM((CH, CH), F32)
    return pl.pallas_call(
        network_kernel,
        out_shape=jax.ShapeDtypeStruct((1, LANES), F32),
        in_specs=[ANY, ANY, VMEM],
        out_specs=VMEM,
        scratch_shapes=[
            block,
            block,
            block,
            pltpu.VMEM(pair_bins.shape[1:], jnp.int32),
            pltpu.VMEM((3, CH, CH), BF16),
            pltpu.VMEM((2, CH, CH), BF16),
            pltpu.VMEM((CH, CH), BF16),
            pltpu.VMEM((freqs, 2, CH, LANES), BF16),
            pltpu.VMEM((2, freqs, 1, EARLY, LANES), BF16),
            pltpu.VMEM((2, freqs, 2, EARLY, LANES), BF16),
            pltpu.VMEM((CH * (freqs + PAD), LANES), F32),
            pltpu.VMEM((2, 2 * freqs * (CH + PAD), LANES), F32),
            square,
            square,
            pltpu.VMEM((SEGMENTS, 2 * freqs, CLASSES), F32),
            pltpu.VMEM((16, CLASSES), F32),
            pltpu.VMEM((NEAR, FAR + COUNT_ROWS, LANES), F32),
            pltpu.VMEM((NEAR - 1, FAR + COUNT_ROWS, LANES), F32),
            pltpu.VMEM((FAR, 1, 2 * LANES), F32),
            pltpu.VMEM((FAR - 1, 1, 2 * LANES), F32),
            DMA((2,)),
            DMA((7,)),
            DMA((7,)),
            DMA((NEAR - 1,)),
            DMA((NEAR - 1,)),
            DMA((FAR - 1,)),
            DMA((FAR - 1,)),
        ],
        compiler_params=pltpu.CompilerParams(
            collective_id=0, has_side_effects=True, vmem_limit_bytes=60 * 1024 * 1024
        ),
    )(spectra, pair_bins, lag_tables(lax.axis_size("off"), freqs, LANES))


def solution(mesh):
    in_specs = (P("chan", "off", None), P("chan", None, None, None))
    out_specs = P(("chan", "off"), None)
    return jax.shard_map(
        on_device, mesh=mesh, in_specs=in_specs, out_specs=out_specs, check_vma=False
    )
```

time: 176 us -> 72.8 us (0.41)
  waiting for transfers between devices: 103 us -> 0 us
  Pallas kernels: 57.5 us -> 71.5 us
  starting transfers between devices: 10.5 us -> 0 us
  local copies, waits for them, and re-layouts: 4.62 us -> 1.19 us
    ppermute x2 -> x0, waiting for transfers between devices: 103 us -> none  [from_ahead(): return lax.ppermute(value, 'chan', pairs)]
    pallas_call x4 -> x1, Pallas kernels: 57.5 us -> 71.5 us  [on_device(): pl.pallas_call(network_kernel, out_shape=jax.ShapeDtypeStruct((1, LANES),...]
    ppermute x2 -> x0, starting transfers between devices: 10.5 us -> none  [from_ahead(): return lax.ppermute(value, 'chan', pairs)]
    unnamed x5 -> x1, local copies, waits for them, and re-layouts: 3.46 us -> 1.19 us
  transfers between devices with their start and end apart: 2 -> 0, of which waited for: 2 -> 0; matrix products, arithmetic and copies ran while one was open for 1% -> 0% of each run, Pallas kernels for 14% -> 0%
where the time goes in v6:
time: 72.8 us; the launch traced here: 72.7 us
  Pallas kernels  71.5 us (98%)
  local copies, waits for them, and re-layouts  1.19 us (2%)
    pallas_call x1, Pallas kernels, on_device(): pl.pallas_call(network_kernel, out_shape=jax.ShapeDtypeStruct((1, LANES),...  71.5 us

profile of v6, /device:TPU:1, one launch (start us, length us, event | category | flops | bytes accessed | tf_op | source)
XLA Modules:
  0.0 72.7 jit_solution(317249693359836365)
XLA Ops:
  0.0 71.5 %shard_map.37 = f32[1,128]{1,0:T(1,128)} custom-call(bf16[256,32,128]{2,1,0:T(8,128)(2,1)} %spectra.1, s32[1,3,256,256]{3,2,1,0:T(8,128)} %pair_bins.1, f32[4,64,128]{2,1,0:T(8,128)} %constant.2.clone.table), custom_call_target="tpu_custom_call" | custom-call | tf_op jit(solution)/shard_map/pallas_call | solution.py:437
  71.5 1.2 %copy.5 = f32[1,128]{1,0:T(1,128)} copy(f32[1,128]{1,0:T(1,128)} %shard_map.37) | data formatting | bytes 1024

commit v7 on v6

--- a/solution.py
+++ b/solution.py
@@ -156,7 +156,7 @@
 def network_kernel(
     spectra, pair_bins, table, out,
     raw, across_raw, beside_raw, labels, sent_labels, across_labels, beside_labels, white, across, beside,
-    rows, cross, slots, segments, sums, tally, parts, near_in, far_out, far_in,
+    rows, cross, slots, segments, sums, mate_sums, tally, parts, near_in, far_out, far_in,
     local_sem, send_sem, recv_sem, near_send, near_recv, far_send, far_recv,
 ):
     freqs = raw.shape[1]
@@ -169,6 +169,7 @@
     near = off * 2 + low
     target = lax.rem(chan + count - 2 + 4 * core, count)
     partner = chan + 1 - 2 * low
+    mate = off + 1 - 2 * core
 
     def near_device(step):
         index = lax.rem(near + step, NEAR)
@@ -208,19 +209,20 @@
 
     pl.semaphore_wait(barrier, FAR - 1 + NEAR - 1)
 
-    def remote(index, source, landing, chan_to):
+    def remote(index, source, landing, chan_to, off_to=off):
         return pltpu.make_async_remote_copy(
             src_ref=source,
             dst_ref=landing,
             send_sem=send_sem.at[index],
             recv_sem=recv_sem.at[index],
-            device_id=(chan_to, off),
+            device_id=(chan_to, off_to),
             device_id_type=MESH,
         )
 
     pieces = [slice(piece * EARLY, (piece + 1) * EARLY) for piece in range(2)]
     across_copies = [remote(i, spectra.at[part], across_raw.at[part], target) for i, part in enumerate(pieces)]
     beside_copies = [remote(2 + i, spectra.at[part], beside_raw.at[part], partner) for i, part in enumerate(pieces)]
+    mate_copies = [remote(7 + i, spectra.at[part], beside_raw.at[part], chan, mate) for i, part in enumerate(pieces)]
     beside_copies.append(remote(4, sent_labels.at[2], beside_labels, partner))
     two_copy = remote(5, sent_labels.at[1], across_labels.at[1], target)
     one_copy = remote(6, sent_labels.at[0], across_labels.at[0], target)
@@ -231,6 +233,11 @@
         beside_copies[0].start()
         beside_copies[2].start()
 
+    @pl.when(heavy)
+    def _():
+        for copy in mate_copies:
+            copy.start()
+
     @pl.when(core == 1)
     def _():
         two_copy.start()
@@ -241,6 +248,7 @@
 
     place_marks(labels[0], 2, slots, segments)
     sums[...] = jnp.zeros_like(sums)
+    mate_sums[...] = jnp.zeros_like(mate_sums)
     tally[...] = jnp.zeros_like(tally)
     load_raw.wait()
     whiten(raw, rows, white, True)
@@ -248,11 +256,20 @@
     def own(freq):
         return white[freq].reshape(2 * CH, LANES)
 
-    def add_tally(segment, values):
-        tally[segment : segment + 1, :] += values
+    def add_tally(weight):
+        def add(segment, values):
+            tally[segment : segment + 1, :] += values * weight
+
+        return add
 
     def add_self(segment, values):
         sums[segment] += values
+
+    def add_mate(segment, values):
+        mate_sums[segment] += values
+
+    counted = (off == 0).astype(F32)
+    counted_self = (off < 2).astype(F32)
 
     sign = (1 - 2 * core).astype(F32)
 
@@ -262,20 +279,33 @@
 
     def bin_pairs(marks):
         place_marks(marks, 2, slots, segments)
-        add_all_bins(cross, slots, segments, 2, (0, 1), 2 * freqs, add_pairs, add_tally)
-
-    cross_pairs(own, lambda freq: white[freq, 0], cross, freqs)
-    bin_self = functools.partial(
-        add_all_bins, cross, slots, segments, 2, (0, 1), 2 * freqs, add_self, add_tally
-    )
-    bin_self(begin=0, end=CH // 2)
-    across_copies[1].start()
+        add_all_bins(cross, slots, segments, 2, (0, 1), 2 * freqs, add_pairs, add_tally(counted))
+
+    def whole(block, row):
+        return lambda freq: jnp.concatenate([block[0, freq, row], block[1, freq, row]], axis=0)
+
+    def beside_rows(freq):
+        return jnp.concatenate([whole(beside, 0)(freq), whole(beside, 1)(freq)], axis=0)
+
+    @pl.when(heavy)
+    def _():
+        across_copies[0].wait_send()
+        across_copies[1].start()
 
     @pl.when(light)
     def _():
+        cross_pairs(own, lambda freq: white[freq, 0], cross, freqs)
+        bin_block = functools.partial(add_all_bins, cross, slots, segments, 2, (0, 1), 2 * freqs)
+        bin_block(add_self, add_tally(counted_self), begin=0, end=CH // 2)
+        across_copies[1].start()
         beside_copies[1].start()
-
-    bin_self(begin=CH // 2, end=CH)
+        bin_block(add_self, add_tally(counted_self), begin=CH // 2, end=CH)
+        for piece, copy in enumerate(mate_copies):
+            copy.wait_recv()
+            whiten(beside_raw.at[pieces[piece]], rows, beside.at[piece], True)
+        cross_pairs(beside_rows, whole(beside, 0), cross, freqs)
+        bin_block(add_mate, add_tally(0.0))
+
     across_copies[0].wait_recv()
     whiten(across_raw.at[pieces[0]], rows, across.at[0], False)
 
@@ -292,12 +322,6 @@
 
     def half_blocks(piece):
         return lambda freq: jnp.concatenate([beside[piece, freq, 0], across[piece, freq, 0]], axis=0)
-
-    def whole(block, row):
-        return lambda freq: jnp.concatenate([block[0, freq, row], block[1, freq, row]], axis=0)
-
-    def beside_rows(freq):
-        return jnp.concatenate([whole(beside, 0)(freq), whole(beside, 1)(freq)], axis=0)
 
     @pl.when(heavy)
     def _():
@@ -329,16 +353,16 @@
         cross_pairs(own, whole(across, 0), cross, freqs)
         bin_pairs(as_integers(across_labels[1]))
 
-    counted = (off == 0).astype(F32)
+    tables = jnp.concatenate([table[off], table[mate]], axis=0)
     for segment in range(SEGMENTS):
         trace = lax.dot_general(
-            sums[segment],
-            table[off],
+            jnp.concatenate([sums[segment], mate_sums[segment]], axis=0),
+            tables,
             (((0,), (0,)), ((), ())),
             precision=lax.Precision.HIGHEST,
             preferred_element_type=F32,
         )
-        counts = jnp.broadcast_to(tally[segment : segment + 1, :] * counted, (COUNT_ROWS, CLASSES))
+        counts = jnp.broadcast_to(tally[segment : segment + 1, :], (COUNT_ROWS, CLASSES))
         counts = jnp.concatenate([counts, jnp.zeros((COUNT_ROWS, LANES - CLASSES), F32)], axis=1)
         for part in range(2):
             parts[segment * 2 + part, :FAR, :] = trace[part * FAR : (part + 1) * FAR]
@@ -404,12 +428,17 @@
 
     lax.fori_loop(1, NEAR, end_near, 0)
     lax.fori_loop(1, FAR, end_far, 0)
-    for copy in across_copies:
-        copy.wait_send()
+    across_copies[1].wait_send()
 
     @pl.when(light)
     def _():
+        across_copies[0].wait_send()
         for copy in beside_copies:
+            copy.wait_send()
+
+    @pl.when(heavy)
+    def _():
+        for copy in mate_copies:
             copy.wait_send()
 
     @pl.when(core == 1)
@@ -455,14 +484,15 @@
             square,
             square,
             pltpu.VMEM((SEGMENTS, 2 * freqs, CLASSES), F32),
+            pltpu.VMEM((SEGMENTS, 2 * freqs, CLASSES), F32),
             pltpu.VMEM((16, CLASSES), F32),
             pltpu.VMEM((NEAR, FAR + COUNT_ROWS, LANES), F32),
             pltpu.VMEM((NEAR - 1, FAR + COUNT_ROWS, LANES), F32),
             pltpu.VMEM((FAR, 1, 2 * LANES), F32),
             pltpu.VMEM((FAR - 1, 1, 2 * LANES), F32),
             DMA((2,)),
-            DMA((7,)),
-            DMA((7,)),
+            DMA((9,)),
+            DMA((9,)),
             DMA((NEAR - 1,)),
             DMA((NEAR - 1,)),
             DMA((FAR - 1,)),

time: 72.8 us -> 73.7 us (1.012)
  Pallas kernels: 71.5 us -> 72.4 us
    pallas_call x1, Pallas kernels: 71.5 us -> 72.4 us  [on_device(): pl.pallas_call(network_kernel, out_shape=jax.ShapeDtypeStruct((1, LANES),...]
where the time goes in v7:
time: 73.7 us; the launch traced here: 73.6 us
  Pallas kernels  72.4 us (98%)
  local copies, waits for them, and re-layouts  1.19 us (2%)
    pallas_call x1, Pallas kernels, on_device(): pl.pallas_call(network_kernel, out_shape=jax.ShapeDtypeStruct((1, LANES),...  72.4 us

profile of v7, /device:TPU:1, one launch (start us, length us, event | category | flops | bytes accessed | tf_op | source)
XLA Modules:
  0.0 73.6 jit_solution(7577161110826569960)
XLA Ops:
  0.0 72.4 %shard_map.37 = f32[1,128]{1,0:T(1,128)} custom-call(bf16[256,32,128]{2,1,0:T(8,128)(2,1)} %spectra.1, s32[1,3,256,256]{3,2,1,0:T(8,128)} %pair_bins.1, f32[4,64,128]{2,1,0:T(8,128)} %constant.2.clone.table), custom_call_target="tpu_custom_call" | custom-call | tf_op jit(solution)/shard_map/pallas_call | solution.py:466
  72.4 1.2 %copy.5 = f32[1,128]{1,0:T(1,128)} copy(f32[1,128]{1,0:T(1,128)} %shard_map.37) | data formatting | bytes 1024

commit v8 on v7

--- a/solution.py
+++ b/solution.py
@@ -19,6 +19,7 @@
 CH = 256
 LANES = 128
 EARLY = CH // 2
+LATE = CH // 4
 HALF = LANES // 2
 SEGMENTS = 4
 CLASSES = 64
@@ -219,19 +220,20 @@
             device_id_type=MESH,
         )
 
-    pieces = [slice(piece * EARLY, (piece + 1) * EARLY) for piece in range(2)]
+    halves = [slice(piece * EARLY, (piece + 1) * EARLY) for piece in range(2)]
+    pieces = [slice(0, EARLY), slice(EARLY, EARLY + LATE), slice(EARLY + LATE, CH)]
     across_copies = [remote(i, spectra.at[part], across_raw.at[part], target) for i, part in enumerate(pieces)]
-    beside_copies = [remote(2 + i, spectra.at[part], beside_raw.at[part], partner) for i, part in enumerate(pieces)]
-    mate_copies = [remote(7 + i, spectra.at[part], beside_raw.at[part], chan, mate) for i, part in enumerate(pieces)]
-    beside_copies.append(remote(4, sent_labels.at[2], beside_labels, partner))
-    two_copy = remote(5, sent_labels.at[1], across_labels.at[1], target)
-    one_copy = remote(6, sent_labels.at[0], across_labels.at[0], target)
+    beside_copies = [remote(3 + i, spectra.at[part], beside_raw.at[part], partner) for i, part in enumerate(pieces)]
+    mate_copies = [remote(9 + i, spectra.at[part], beside_raw.at[part], chan, mate) for i, part in enumerate(halves)]
+    beside_copies.append(remote(6, sent_labels.at[2], beside_labels, partner))
+    two_copy = remote(7, sent_labels.at[1], across_labels.at[1], target)
+    one_copy = remote(8, sent_labels.at[0], across_labels.at[0], target)
     across_copies[0].start()
 
     @pl.when(light)
     def _():
         beside_copies[0].start()
-        beside_copies[2].start()
+        beside_copies[3].start()
 
     @pl.when(heavy)
     def _():
@@ -279,7 +281,8 @@
 
     def bin_pairs(marks):
         place_marks(marks, 2, slots, segments)
-        add_all_bins(cross, slots, segments, 2, (0, 1), 2 * freqs, add_pairs, add_tally(counted))
+        sides = tuple(range(marks.shape[1] // LANES))
+        add_all_bins(cross, slots, segments, 2, sides, 2 * freqs, add_pairs, add_tally(counted))
 
     def whole(block, row):
         return lambda freq: jnp.concatenate([block[0, freq, row], block[1, freq, row]], axis=0)
@@ -296,14 +299,15 @@
     def _():
         cross_pairs(own, lambda freq: white[freq, 0], cross, freqs)
         bin_block = functools.partial(add_all_bins, cross, slots, segments, 2, (0, 1), 2 * freqs)
-        bin_block(add_self, add_tally(counted_self), begin=0, end=CH // 2)
+        bin_block(add_self, add_tally(counted_self))
         across_copies[1].start()
         beside_copies[1].start()
-        bin_block(add_self, add_tally(counted_self), begin=CH // 2, end=CH)
         for piece, copy in enumerate(mate_copies):
             copy.wait_recv()
-            whiten(beside_raw.at[pieces[piece]], rows, beside.at[piece], True)
+            whiten(beside_raw.at[halves[piece]], rows, beside.at[piece], True)
         cross_pairs(beside_rows, whole(beside, 0), cross, freqs)
+        across_copies[2].start()
+        beside_copies[2].start()
         bin_block(add_mate, add_tally(0.0))
 
     across_copies[0].wait_recv()
@@ -316,30 +320,40 @@
     def beside_marks():
         return jnp.where(core == 0, labels[1], as_integers(beside_labels[...]))
 
-    def half_marks(piece):
-        lanes = slice(piece * LANES, (piece + 1) * LANES)
-        return jnp.concatenate([beside_marks()[:, lanes], as_integers(across_labels[1])[:, lanes]], axis=1)
-
-    def half_blocks(piece):
-        return lambda freq: jnp.concatenate([beside[piece, freq, 0], across[piece, freq, 0]], axis=0)
+    def piece_marks(part):
+        return jnp.concatenate([beside_marks()[:, part], as_integers(across_labels[1])[:, part]], axis=1)
+
+    def late_part(piece):
+        return pl.ds((piece - 1) * LATE, LATE)
+
+    def whiten_across(piece):
+        across_copies[piece].wait_recv()
+        whiten(across_raw.at[pieces[piece]], rows, across.at[1, :, :, late_part(piece), :], False)
 
     @pl.when(heavy)
     def _():
         beside_copies[0].wait_recv()
-        beside_copies[2].wait_recv()
+        beside_copies[3].wait_recv()
         whiten(beside_raw.at[pieces[0]], rows, beside.at[0], True)
-        cross_pairs(own, half_blocks(0), cross, freqs)
-        bin_pairs(half_marks(0))
-
-    across_copies[1].wait_recv()
-    whiten(across_raw.at[pieces[1]], rows, across.at[1], False)
-
-    @pl.when(heavy)
-    def _():
-        beside_copies[1].wait_recv()
-        whiten(beside_raw.at[pieces[1]], rows, beside.at[1], True)
-        cross_pairs(own, half_blocks(1), cross, freqs)
-        bin_pairs(half_marks(1))
+        cross_pairs(
+            own, lambda freq: jnp.concatenate([beside[0, freq, 0], across[0, freq, 0]], axis=0), cross, freqs
+        )
+        across_copies[2].start()
+        bin_pairs(piece_marks(pieces[0]))
+        for piece in (1, 2):
+            part = late_part(piece)
+            whiten_across(piece)
+            beside_copies[piece].wait_recv()
+            whiten(beside_raw.at[pieces[piece]], rows, beside.at[1, :, :, part, :], True)
+            cross_pairs(
+                own,
+                lambda freq, part=part: jnp.concatenate(
+                    [beside[1, freq, 0, part, :], across[1, freq, 0, part, :]], axis=0
+                ),
+                cross,
+                freqs,
+            )
+            bin_pairs(piece_marks(pieces[piece]))
 
         @pl.when(core == 1)
         def _():
@@ -350,6 +364,8 @@
 
     @pl.when(light)
     def _():
+        whiten_across(1)
+        whiten_across(2)
         cross_pairs(own, whole(across, 0), cross, freqs)
         bin_pairs(as_integers(across_labels[1]))
 
@@ -429,6 +445,7 @@
     lax.fori_loop(1, NEAR, end_near, 0)
     lax.fori_loop(1, FAR, end_far, 0)
     across_copies[1].wait_send()
+    across_copies[2].wait_send()
 
     @pl.when(light)
     def _():
@@ -491,8 +508,8 @@
             pltpu.VMEM((FAR, 1, 2 * LANES), F32),
             pltpu.VMEM((FAR - 1, 1, 2 * LANES), F32),
             DMA((2,)),
-            DMA((9,)),
-            DMA((9,)),
+            DMA((11,)),
+            DMA((11,)),
             DMA((NEAR - 1,)),
             DMA((NEAR - 1,)),
             DMA((FAR - 1,)),

time: 73.7 us -> 74.9 us (1.016)
  Pallas kernels: 72.4 us -> 73.6 us
    pallas_call x1, Pallas kernels: 72.4 us -> 73.6 us  [on_device(): pl.pallas_call(network_kernel, out_shape=jax.ShapeDtypeStruct((1, LANES),...]
where the time goes in v8:
time: 74.9 us; the launch traced here: 74.8 us
  Pallas kernels  73.6 us (98%)
  local copies, waits for them, and re-layouts  1.19 us (2%)
    pallas_call x1, Pallas kernels, on_device(): pl.pallas_call(network_kernel, out_shape=jax.ShapeDtypeStruct((1, LANES),...  73.6 us

profile of v8, /device:TPU:1, one launch (start us, length us, event | category | flops | bytes accessed | tf_op | source)
XLA Modules:
  0.0 74.8 jit_solution(16885123476309605958)
XLA Ops:
  0.0 73.6 %shard_map.37 = f32[1,128]{1,0:T(1,128)} custom-call(bf16[256,32,128]{2,1,0:T(8,128)(2,1)} %spectra.1, s32[1,3,256,256]{3,2,1,0:T(8,128)} %pair_bins.1, f32[4,64,128]{2,1,0:T(8,128)} %constant.2.clone.table), custom_call_target="tpu_custom_call" | custom-call | tf_op jit(solution)/shard_map/pallas_call | solution.py:483
  73.6 1.2 %copy.5 = f32[1,128]{1,0:T(1,128)} copy(f32[1,128]{1,0:T(1,128)} %shard_map.37) | data formatting | bytes 1024

commit v9 on v8

--- a/solution.py
+++ b/solution.py
@@ -221,19 +221,19 @@
         )
 
     halves = [slice(piece * EARLY, (piece + 1) * EARLY) for piece in range(2)]
-    pieces = [slice(0, EARLY), slice(EARLY, EARLY + LATE), slice(EARLY + LATE, CH)]
+    pieces = [slice(piece * LATE, (piece + 1) * LATE) for piece in range(4)]
     across_copies = [remote(i, spectra.at[part], across_raw.at[part], target) for i, part in enumerate(pieces)]
-    beside_copies = [remote(3 + i, spectra.at[part], beside_raw.at[part], partner) for i, part in enumerate(pieces)]
-    mate_copies = [remote(9 + i, spectra.at[part], beside_raw.at[part], chan, mate) for i, part in enumerate(halves)]
-    beside_copies.append(remote(6, sent_labels.at[2], beside_labels, partner))
-    two_copy = remote(7, sent_labels.at[1], across_labels.at[1], target)
-    one_copy = remote(8, sent_labels.at[0], across_labels.at[0], target)
+    beside_copies = [remote(4 + i, spectra.at[part], beside_raw.at[part], partner) for i, part in enumerate(pieces)]
+    mate_copies = [remote(11 + i, spectra.at[part], beside_raw.at[part], chan, mate) for i, part in enumerate(halves)]
+    beside_copies.append(remote(8, sent_labels.at[2], beside_labels, partner))
+    two_copy = remote(9, sent_labels.at[1], across_labels.at[1], target)
+    one_copy = remote(10, sent_labels.at[0], across_labels.at[0], target)
     across_copies[0].start()
 
     @pl.when(light)
     def _():
         beside_copies[0].start()
-        beside_copies[3].start()
+        beside_copies[4].start()
 
     @pl.when(heavy)
     def _():
@@ -292,26 +292,27 @@
 
     @pl.when(heavy)
     def _():
+        across_copies[1].start()
         across_copies[0].wait_send()
+        across_copies[2].start()
+
+    @pl.when(light)
+    def _():
         across_copies[1].start()
-
-    @pl.when(light)
-    def _():
+        beside_copies[1].start()
         cross_pairs(own, lambda freq: white[freq, 0], cross, freqs)
         bin_block = functools.partial(add_all_bins, cross, slots, segments, 2, (0, 1), 2 * freqs)
-        bin_block(add_self, add_tally(counted_self))
-        across_copies[1].start()
-        beside_copies[1].start()
+        bin_block(add_self, add_tally(counted_self), begin=0, end=CH // 2)
+        across_copies[2].start()
+        beside_copies[2].start()
+        bin_block(add_self, add_tally(counted_self), begin=CH // 2, end=CH)
+        across_copies[3].start()
+        beside_copies[3].start()
         for piece, copy in enumerate(mate_copies):
             copy.wait_recv()
             whiten(beside_raw.at[halves[piece]], rows, beside.at[piece], True)
         cross_pairs(beside_rows, whole(beside, 0), cross, freqs)
-        across_copies[2].start()
-        beside_copies[2].start()
         bin_block(add_mate, add_tally(0.0))
-
-    across_copies[0].wait_recv()
-    whiten(across_raw.at[pieces[0]], rows, across.at[0], False)
 
     @pl.when(core == 1)
     def _():
@@ -323,36 +324,32 @@
     def piece_marks(part):
         return jnp.concatenate([beside_marks()[:, part], as_integers(across_labels[1])[:, part]], axis=1)
 
-    def late_part(piece):
-        return pl.ds((piece - 1) * LATE, LATE)
+    def place_of(piece):
+        return piece // 2, pl.ds(piece % 2 * LATE, LATE)
 
     def whiten_across(piece):
+        side, part = place_of(piece)
         across_copies[piece].wait_recv()
-        whiten(across_raw.at[pieces[piece]], rows, across.at[1, :, :, late_part(piece), :], False)
+        whiten(across_raw.at[pieces[piece]], rows, across.at[side, :, :, part, :], False)
 
     @pl.when(heavy)
     def _():
-        beside_copies[0].wait_recv()
-        beside_copies[3].wait_recv()
-        whiten(beside_raw.at[pieces[0]], rows, beside.at[0], True)
-        cross_pairs(
-            own, lambda freq: jnp.concatenate([beside[0, freq, 0], across[0, freq, 0]], axis=0), cross, freqs
-        )
-        across_copies[2].start()
-        bin_pairs(piece_marks(pieces[0]))
-        for piece in (1, 2):
-            part = late_part(piece)
+        beside_copies[4].wait_recv()
+        for piece in range(4):
+            side, part = place_of(piece)
             whiten_across(piece)
             beside_copies[piece].wait_recv()
-            whiten(beside_raw.at[pieces[piece]], rows, beside.at[1, :, :, part, :], True)
+            whiten(beside_raw.at[pieces[piece]], rows, beside.at[side, :, :, part, :], True)
             cross_pairs(
                 own,
-                lambda freq, part=part: jnp.concatenate(
-                    [beside[1, freq, 0, part, :], across[1, freq, 0, part, :]], axis=0
+                lambda freq, side=side, part=part: jnp.concatenate(
+                    [beside[side, freq, 0, part, :], across[side, freq, 0, part, :]], axis=0
                 ),
                 cross,
                 freqs,
             )
+            if piece == 0:
+                across_copies[3].start()
             bin_pairs(piece_marks(pieces[piece]))
 
         @pl.when(core == 1)
@@ -364,8 +361,8 @@
 
     @pl.when(light)
     def _():
-        whiten_across(1)
-        whiten_across(2)
+        for piece in range(4):
+            whiten_across(piece)
         cross_pairs(own, whole(across, 0), cross, freqs)
         bin_pairs(as_integers(across_labels[1]))
 
@@ -446,6 +443,7 @@
     lax.fori_loop(1, FAR, end_far, 0)
     across_copies[1].wait_send()
     across_copies[2].wait_send()
+    across_copies[3].wait_send()
 
     @pl.when(light)
     def _():
@@ -508,8 +506,8 @@
             pltpu.VMEM((FAR, 1, 2 * LANES), F32),
             pltpu.VMEM((FAR - 1, 1, 2 * LANES), F32),
             DMA((2,)),
-            DMA((11,)),
-            DMA((11,)),
+            DMA((13,)),
+            DMA((13,)),
             DMA((NEAR - 1,)),
             DMA((NEAR - 1,)),
             DMA((FAR - 1,)),

time: 74.9 us -> 71.4 us (0.953)
  Pallas kernels: 73.6 us -> 70.1 us
    pallas_call x1, Pallas kernels: 73.6 us -> 70.1 us  [on_device(): pl.pallas_call(network_kernel, out_shape=jax.ShapeDtypeStruct((1, LANES),...]
where the time goes in v9:
time: 71.4 us; the launch traced here: 71.3 us
  Pallas kernels  70.1 us (98%)
  local copies, waits for them, and re-layouts  1.19 us (2%)
    pallas_call x1, Pallas kernels, on_device(): pl.pallas_call(network_kernel, out_shape=jax.ShapeDtypeStruct((1, LANES),...  70.1 us

profile of v9, /device:TPU:1, one launch (start us, length us, event | category | flops | bytes accessed | tf_op | source)
XLA Modules:
  0.0 71.3 jit_solution(10755663325902825357)
XLA Ops:
  0.0 70.1 %shard_map.37 = f32[1,128]{1,0:T(1,128)} custom-call(bf16[256,32,128]{2,1,0:T(8,128)(2,1)} %spectra.1, s32[1,3,256,256]{3,2,1,0:T(8,128)} %pair_bins.1, f32[4,64,128]{2,1,0:T(8,128)} %constant.2.clone.table), custom_call_target="tpu_custom_call" | custom-call | tf_op jit(solution)/shard_map/pallas_call | solution.py:481
  70.1 1.2 %copy.5 = f32[1,128]{1,0:T(1,128)} copy(f32[1,128]{1,0:T(1,128)} %shard_map.37) | data formatting | bytes 1024
